TPU v7x, 256 devices: a whole 4x4x8 slice. The times are simulated.
256 devices in a mesh: group: 4 (over z_hi), resp: 16 (over z_lo, y, core), tensor: 4 (over x).
Axes of the slice: x: 4, y: 4, z: 8 (z_hi: 4, z_lo: 2; z = z_hi * 2 + z_lo), core: 2. Of those that a mesh axis runs over, the one named last changes fastest.
Arguments:
- prompt_rotated_keys: bfloat16 [16384, 1024], P(('group', 'resp'), 'tensor'), parts along dimension 0, may hold values from -420 to 420
- prompt_value_cache: bfloat16 [16384, 1024], P(('group', 'resp'), 'tensor'), parts along dimension 0, may hold values from -6 to 6
- queries: bfloat16 [16384, 8192], P(('group', 'resp', 'tensor')), parts along dimension 0, may hold values from -6 to 6
- response_keys: bfloat16 [16384, 1024], P(('group', 'resp', 'tensor')), parts along dimension 0, may hold values from -6 to 6
- response_values: bfloat16 [16384, 1024], P(('group', 'resp', 'tensor')), parts along dimension 0, may hold values from -6 to 6
- q_gain: float32 [128], replicated, may hold values from 1 to 2
- key_norm_gain: float32 [128], replicated, may hold values from 1 to 2
- prompt_len: int32 [4], P('group'), parts along dimension 0, may hold values from 1024 to 4096
- resp_len: int32 [64], P(('group', 'resp')), parts along dimension 0, may hold values from 64 to 256, as said below
Outputs:
- attended: bfloat16 [16384, 8192], P(('group', 'resp', 'tensor')), parts along dimension 0
There are 4 independent parts, one for each index of `group`. A program takes and returns all parts, laid end to end along the dimension named above; an argument that names none is the same for every part. Nothing has to cross between parts.
Inputs may be any that keep to these rules, and one draw needn't show every extreme that they name: `resp_len`: exactly one response has 256 live positions, the others fewer.
All inputs are finite; a program needn't handle non-finite values.
Results may differ from a plain program's by a relative error of at most 0.014.
Values may be sent and summed in bfloat16 or wider, within the bound.
No kernel may reach another device: no remote copies, remote signals or barrier semaphores. Data moves between devices by JAX's collectives and lax.ppermute only.
A program may use at most 128 MiB of HBM per device.

v0:
```python
import functools

import jax
import jax.numpy as jnp
from jax import lax
from jax.experimental import pallas as pl
from jax.experimental.pallas import tpu as pltpu
from jax.sharding import PartitionSpec as P

HEAD = 128
LENGTH = 256
ROWS = 1024
CHUNK = 1024
LOG2E = 1.4426950408889634
NEG = -1e30
MIB = 1024 * 1024


def nt(a, b):
    return lax.dot_general(a, b, (((1,), (1,)), ((), ())), preferred_element_type=jnp.float32)


def mm(a, b):
    return jnp.dot(a, b, preferred_element_type=jnp.float32)


def split_kernel(meta, pk, pv, queries, rk, rv, own, q1, q2, q3, kv):
    t = meta[0]
    for d, dst in enumerate((own, q1, q2, q3)):
        u = lax.rem(t + d, 4)
        dst[:, :2048] = queries[:, pl.ds(pl.multiple_of(u * 2048, 2048), 2048)]
        dst[:, 2048:2304] = rk[:, pl.ds(pl.multiple_of(u * 256, 256), 256)]
        dst[:, 2304:] = rv[:, pl.ds(pl.multiple_of(u * 256, 256), 256)]
    for h in range(2):
        kv[:, h * 256 : h * 256 + 128] = pk[:, h * 128 : (h + 1) * 128]
        kv[:, h * 256 + 128 : h * 256 + 256] = pv[:, h * 128 : (h + 1) * 128]


def split(meta, *args):
    vmem = pl.BlockSpec(memory_space=pltpu.VMEM)
    piece = jax.ShapeDtypeStruct((64, 2560), jnp.bfloat16)
    return pl.pallas_call(
        split_kernel,
        out_shape=(piece,) * 4 + (jax.ShapeDtypeStruct((256, 512), jnp.bfloat16),),
        in_specs=[pl.BlockSpec(memory_space=pltpu.SMEM)] + [vmem] * 5,
        out_specs=(vmem,) * 5,
        compiler_params=pltpu.CompilerParams(vmem_limit_bytes=16 * MIB),
        name="split",
    )(meta, *args)


def prep_kernel(meta, own, r1, r2, r3, aq, bq, ak, bk, q0, q1, rkv):
    t = meta[0]
    wide = jnp.ones((256, 128), jnp.bfloat16)
    at = lax.broadcasted_iota(jnp.int32, (128, 128), 0)
    to = lax.broadcasted_iota(jnp.int32, (128, 128), 1)
    swap = jnp.where((at - to == 64) | (to - at == 64), 1.0, 0.0).astype(jnp.bfloat16)

    def rotated(x, a, b):
        f = x.astype(jnp.float32)
        sq = f * f
        hi = sq.astype(jnp.bfloat16)
        lo = (sq - hi.astype(jnp.float32)).astype(jnp.bfloat16)
        total = mm(jnp.concatenate([hi, lo], axis=1), wide)
        r = lax.rsqrt(total * (1.0 / HEAD) + 1e-06)
        return ((f * a + mm(x, swap) * b) * r).astype(jnp.bfloat16)

    for d, piece in enumerate((own, r1, r2, r3)):
        s = lax.rem(t - d + 4, 4)
        p0 = pl.multiple_of(s * 64, 64)
        rows = pl.ds(p0, 64)
        base = (s // 2) * ROWS + lax.rem(s, 2) * 64
        a8 = jnp.concatenate([aq[rows, :]] * 8, axis=0)
        b8 = jnp.concatenate([bq[rows, :]] * 8, axis=0)
        for h, dst in enumerate((q0, q1)):
            x = jnp.concatenate(
                [piece[:, (h * 8 + j) * 128 : (h * 8 + j + 1) * 128] for j in range(8)], axis=0
            )
            y = rotated(x, a8, b8)
            for j in range(8):
                dst[pl.ds(pl.multiple_of(base + j * 128, 64), 64), :] = y[j * 64 : (j + 1) * 64]
            k = piece[:, 2048 + h * 128 : 2048 + (h + 1) * 128]
            rkv[rows, h * 256 : h * 256 + 128] = rotated(k, ak[rows, :], bk[rows, :])
            rkv[rows, h * 256 + 128 : h * 256 + 256] = piece[
                :, 2304 + h * 128 : 2304 + (h + 1) * 128
            ]


def prep(meta, pieces, tables):
    vmem = pl.BlockSpec(memory_space=pltpu.VMEM)
    return pl.pallas_call(
        prep_kernel,
        out_shape=(
            jax.ShapeDtypeStruct((2048, 128), jnp.bfloat16),
            jax.ShapeDtypeStruct((2048, 128), jnp.bfloat16),
            jax.ShapeDtypeStruct((256, 512), jnp.bfloat16),
        ),
        in_specs=[pl.BlockSpec(memory_space=pltpu.SMEM)] + [vmem] * 8,
        out_specs=(vmem,) * 3,
        compiler_params=pltpu.CompilerParams(vmem_limit_bytes=16 * MIB),
        cost_estimate=pl.CostEstimate(flops=10**9, bytes_accessed=3 * 10**6, transcendentals=10**6),
        name="prep",
    )(meta, *pieces, *tables)


def lanes(x, f, start):
    for i in range(x.shape[1] // 128):
        start = f(start, x[:, i * 128 : (i + 1) * 128])
    return start


def attend_kernel(heads, first, last, layout, *refs):
    it = iter(refs)
    meta = next(it)
    qs = [next(it) for _ in heads]
    rkv = next(it) if first else None
    pieces = [next(it) for _ in layout]
    states = [[next(it) for _ in range(3)] for _ in heads] if not first else None
    outs = [[next(it) for _ in range(4)] if last else [next(it) for _ in range(3)] for _ in heads]
    kvs, bias, m_s, mx_s, l_s, acc_s, sa, sb, oa, ob, sems = it
    plen, rlen, t, core = meta[0], meta[1], meta[2], meta[3]
    chips = 1 + max(i for i, _, _, _ in layout)
    slots, live = [], 0
    for i in range(chips):
        is_live = (meta[4 + i] < plen).astype(jnp.int32)
        dead = i - live
        slots.append(jnp.where(is_live == 1, live, chips - 1 - dead))
        live = live + is_live
    steps = (live * 512 + CHUNK - 1) // CHUNK
    copies = []
    for n, (piece, (i, other, row, count)) in enumerate(zip(pieces, layout)):
        c = 1 - core if other else core
        to = pl.multiple_of(slots[i] * 512 + c * 256 + row, 128)
        for k, h in enumerate(heads):
            copy = pltpu.make_async_copy(
                piece.at[:, pl.ds(h * 256, 256)],
                kvs.at[k, pl.ds(to, count), :],
                sems.at[n * len(heads) + k],
            )
            copy.start()
            copies.append(copy)
    for i in range(chips):
        at = lax.broadcasted_iota(jnp.int32, (8, 512), 1) + meta[4 + i]
        bias[slots[i]] = jnp.where(at < plen, 0.0, NEG)

    s_bufs, o_bufs = (sa, sb), (oa, ob)
    tiles = [(k, p) for k in range(len(heads)) for p in range(2)]

    def rows_of(p):
        return slice(p * ROWS, (p + 1) * ROWS)

    def begin1(n):
        k, p = tiles[n]
        if first:
            h = heads[k]
            s = nt(qs[k][rows_of(p), :], rkv[:, h * 256 : h * 256 + 128])
            key = lax.broadcasted_iota(jnp.int32, (ROWS, 256), 1)
            pos = p * 128 + lax.rem(lax.broadcasted_iota(jnp.int32, (ROWS, 256), 0), 128)
            s = jnp.where((key <= pos) & (key < rlen), s, NEG)
            o_bufs[n % 2][...] = s
            m_s[...] = jnp.maximum(s[:, :128], s[:, 128:])
        else:
            m_s[...] = states[k][0][rows_of(p), :]

    def pass1(n, c):
        k, p = tiles[n]
        keys = kvs[k, pl.ds(pl.multiple_of(c * CHUNK, CHUNK), CHUNK), 0:128]
        add = jnp.concatenate([bias[2 * c], bias[2 * c + 1]], axis=1)[0:1, :]
        s = nt(qs[k][rows_of(p), :], keys) + add
        s_bufs[n % 2][c] = s
        m_s[...] = lanes(s, jnp.maximum, m_s[...])

    def weigh(s, m):
        return jnp.concatenate(
            [
                jnp.exp2((s[:, i * 128 : (i + 1) * 128] - m) * LOG2E)
                for i in range(s.shape[1] // 128)
            ],
            axis=1,
        )

    def begin2(n):
        k, p = tiles[n]
        m = jnp.broadcast_to(jnp.max(m_s[...], axis=-1, keepdims=True), (ROWS, 128))
        mx_s[...] = m
        if first:
            h = heads[k]
            w = weigh(o_bufs[n % 2][...], m)
            l_s[...] = w[:, :128] + w[:, 128:]
            acc_s[...] = mm(w.astype(jnp.bfloat16), rkv[:, h * 256 + 128 : h * 256 + 256])
        else:
            old = jnp.exp2((states[k][0][rows_of(p), :] - m) * LOG2E)
            l_s[...] = states[k][1][rows_of(p), :] * old
            acc_s[...] = states[k][2][rows_of(p), :] * old

    def pass2(n, c):
        k, _ = tiles[n]
        values = kvs[k, pl.ds(pl.multiple_of(c * CHUNK, CHUNK), CHUNK), 128:256]
        w = weigh(s_bufs[n % 2][c], mx_s[...])
        l_s[...] = lanes(w, jnp.add, l_s[...])
        acc_s[...] += mm(w.astype(jnp.bfloat16), values)

    def finish(n):
        k, p = tiles[n]
        if not last:
            for ref, x in zip(outs[k], (mx_s, l_s, acc_s)):
                ref[rows_of(p), :] = x[...]
            return
        total = jnp.sum(l_s[...], axis=-1, keepdims=True)
        res = acc_s[...] / total
        pos = p * 128 + lax.rem(lax.broadcasted_iota(jnp.int32, (ROWS, 128), 0), 128)
        res = jnp.where(pos < rlen, res, 0.0).astype(jnp.bfloat16)
        for half in range(2):
            d = lax.rem(p * 2 + half - t + 4, 4)
            for e in range(4):

                @pl.when(d == e)
                def _():
                    for j in range(8):
                        r = j * 128 + half * 64
                        outs[k][e][:, j * 128 : (j + 1) * 128] = res[r : r + 64]

    begin1(0)
    for copy in copies:
        copy.wait()

    def loop(f):
        lax.fori_loop(0, steps, lambda c, z: (f(c), z)[1], 0)

    loop(lambda c: pass1(0, c))
    for n in range(len(tiles)):
        begin2(n)
        if n + 1 < len(tiles):
            begin1(n + 1)

            def both(c):
                pass1(n + 1, c)
                pass2(n, c)

            loop(both)
        else:
            loop(lambda c: pass2(n, c))
        finish(n)


def attend(heads, first, last, layout, meta, qs, rkv, pieces, states):
    vmem = pl.BlockSpec(memory_space=pltpu.VMEM)
    anywhere = pl.BlockSpec(memory_space=pl.ANY)
    chips = 1 + max(i for i, _, _, _ in layout)
    state = jax.ShapeDtypeStruct((2048, 128), jnp.float32)
    if last:
        out_shape = [jax.ShapeDtypeStruct((64, 1024), jnp.bfloat16)] * (4 * len(heads))
    else:
        out_shape = [state] * (3 * len(heads))
    steps = chips * 512 // CHUNK
    f32 = jnp.float32
    scratch = [
        pltpu.VMEM((len(heads), chips * 512, 256), jnp.bfloat16),
        pltpu.VMEM((chips, 8, 512), f32),
        *[pltpu.VMEM((ROWS, 128), f32)] * 4,
        *[pltpu.VMEM((steps, ROWS, CHUNK), f32)] * 2,
        *[pltpu.VMEM((ROWS if first else 8, 256), f32)] * 2,
        pltpu.SemaphoreType.DMA((len(layout) * len(heads),)),
    ]
    args = [meta, *qs] + ([rkv] if first else []) + list(pieces)
    specs = [pl.BlockSpec(memory_space=pltpu.SMEM)] + [vmem] * len(qs)
    specs += ([vmem] if first else []) + [anywhere] * len(pieces)
    if not first:
        args += [x for s in states for x in s]
        specs += [vmem] * (3 * len(heads))
    keys = chips * 512 + (256 if first else 0)
    return pl.pallas_call(
        functools.partial(attend_kernel, heads, first, last, layout),
        out_shape=tuple(out_shape),
        in_specs=specs,
        out_specs=(vmem,) * len(out_shape),
        scratch_shapes=scratch,
        compiler_params=pltpu.CompilerParams(vmem_limit_bytes=32 * MIB),
        cost_estimate=pl.CostEstimate(
            flops=8 * 2048 * keys * 128 * len(heads),
            bytes_accessed=4 * MIB,
            transcendentals=2048 * keys * len(heads),
        ),
        name="attend",
    )(*args)


def gather_kernel(meta, *refs):
    pieces, out = refs[:8], refs[8]
    t = meta[0]
    for n, piece in enumerate(pieces):
        h, d = n // 4, n % 4
        to = pl.multiple_of(lax.rem(t - d + 4, 4) * 2048 + h * 1024, 1024)
        out[:, pl.ds(to, 1024)] = piece[...]


def assemble(meta, pieces):
    vmem = pl.BlockSpec(memory_space=pltpu.VMEM)
    return pl.pallas_call(
        gather_kernel,
        out_shape=jax.ShapeDtypeStruct((64, 8192), jnp.bfloat16),
        in_specs=[pl.BlockSpec(memory_space=pltpu.SMEM)] + [vmem] * 8,
        out_specs=vmem,
        compiler_params=pltpu.CompilerParams(vmem_limit_bytes=16 * MIB),
        name="assemble",
    )(meta, *pieces)


def place(z, y, c):
    return z * 8 + y * 2 + c


def move(x, dz, dy, dc=0):
    pairs = [
        (place(z, y, c), place(z ^ dz, (y + dy) % 4, c ^ dc))
        for z in range(2)
        for y in range(4)
        for c in range(2)
    ]
    return lax.ppermute(x, "resp", pairs)


def shift(x, d):
    return lax.ppermute(x, "tensor", [(i, (i + d) % 4) for i in range(4)])


def per_device(pk, pv, queries, rk, rv, q_gain, k_gain, prompt_len, resp_len):
    plen, rlen = prompt_len[0], resp_len[0]
    t = lax.axis_index("tensor")
    r = lax.axis_index("resp")
    core, y, z = r % 2, (r // 2) % 4, r // 8

    *mine, kv = split(jnp.stack([t]), pk, pv, queries, rk, rv)
    q_pieces = [mine[0]] + [shift(mine[d], d) for d in (1, 2, 3)]
    kz, ka, kb, ks = move(kv, 1, 0), move(kv, 0, 1), move(kv, 0, 3), move(kv, 0, 2)
    kza, kzb, kzs = move(kz, 0, 1), move(kz, 0, 3), move(kz, 0, 2)

    half = HEAD // 2
    pos = (plen + jnp.arange(LENGTH, dtype=jnp.int32)).astype(jnp.float32)
    freqs = jnp.power(
        jnp.float32(1000000.0), -jnp.arange(half).astype(jnp.float32) * (2.0 / HEAD)
    )
    angles = pos[:, None] * freqs[None, :]
    cosine, sine = jnp.cos(angles), jnp.sin(angles)
    c2 = jnp.concatenate([cosine, cosine], axis=1)
    s2 = jnp.concatenate([-sine, sine], axis=1)
    scale = HEAD ** (-0.5)
    tables = (
        c2 * (q_gain * scale),
        s2 * (jnp.roll(q_gain, half) * scale),
        c2 * k_gain,
        s2 * jnp.roll(k_gain, half),
    )
    q0, q1, rkv = prep(jnp.stack([t]), q_pieces, tables)

    def base(dz, dy):
        return ((z + dz) % 2 * 4 + (y + dy) % 4) * 512

    def meta(chips):
        return jnp.stack([plen, rlen, t, core] + [base(dz, dy) for dz, dy in chips]).astype(
            jnp.int32
        )

    def both(pieces):
        return list(pieces) + [move(x, 0, 0, 1) for x in pieces]

    layout = [(i, o, 0, 256) for o in range(2) for i in range(4)]
    one = both([kv, kz, ka, kb])
    meta_one = meta([(0, 0), (1, 0), (0, -1), (0, 1)])
    meta_two = meta([(1, -1), (1, 1), (0, 2), (1, 2)])
    st0 = attend((0,), True, False, layout, meta_one, (q0,), rkv, one, None)
    (kza, kzb, ks, kzs), st0 = lax.optimization_barrier(((kza, kzb, ks, kzs), st0))
    two = both([kza, kzb, ks, kzs])
    st1 = attend((1,), True, False, layout, meta_one, (q1,), rkv, one, None)
    pieces = []
    for h, q, st in ((0, q0, st0), (1, q1, st1)):
        o = attend((h,), False, True, layout, meta_two, (q,), None, two, [st])
        pieces += [o[0]] + [shift(o[d], d) for d in (1, 2, 3)]
    return assemble(jnp.stack([t]), pieces)


def solution(mesh):
    rows = P(("group", "resp", "tensor"), None)
    cache = P(("group", "resp"), "tensor")
    in_specs = (cache, cache, rows, rows, rows, P(), P(), P("group"), P(("group", "resp")))
    return jax.shard_map(
        per_device, mesh=mesh, in_specs=in_specs, out_specs=rows, check_vma=False
    )
```

profile of v0, /device:TPU:162, one launch (start us, length us, event | category | flops | bytes accessed | tf_op | source)
XLA Modules:
  0.0 85.5 jit_solution(17470975295956572643)
XLA Ops:
  0.0 1.2 %copy-done = bf16[64,8192]{1,0:T(8,128)(2,1)S(1)} copy-done((bf16[64,8192]{1,0:T(8,128)(2,1)S(1)}, bf16[64,8192]{1,0:T(8,128)(2,1)}, u32[]{:S(2)}) %copy-start) | copy-done | bytes 1048600
  1.2 0.9 %copy-done.1 = bf16[256,256]{1,0:T(8,128)(2,1)S(1)} copy-done((bf16[256,256]{1,0:T(8,128)(2,1)S(1)}, bf16[256,256]{1,0:T(8,128)(2,1)}, u32[]{:S(2)}) %copy-start.1) | copy-done | bytes 131096
  2.1 0.9 %copy-done.2 = bf16[256,256]{1,0:T(8,128)(2,1)S(1)} copy-done((bf16[256,256]{1,0:T(8,128)(2,1)S(1)}, bf16[256,256]{1,0:T(8,128)(2,1)}, u32[]{:S(2)}) %copy-start.2) | copy-done | bytes 131096
  3.0 0.9 %copy-done.3 = bf16[64,1024]{1,0:T(8,128)(2,1)S(1)} copy-done((bf16[64,1024]{1,0:T(8,128)(2,1)S(1)}, bf16[64,1024]{1,0:T(8,128)(2,1)}, u32[]{:S(2)}) %copy-start.3) | copy-done | bytes 131096
  3.9 0.9 %copy-done.4 = bf16[64,1024]{1,0:T(8,128)(2,1)S(1)} copy-done((bf16[64,1024]{1,0:T(8,128)(2,1)S(1)}, bf16[64,1024]{1,0:T(8,128)(2,1)}, u32[]{:S(2)}) %copy-start.4) | copy-done | bytes 131096
  4.8 0.1 split.1
  5.0 3.1 %collective-permute-start.9 = (bf16[256,512]{1,0:T(8,128)(2,1)S(1)}, bf16[256,512]{1,0:T(8,128)(2,1)S(1)}, u32[]{:S(2)}, u32[]{:S(2)}) collective-permute-start(bf16[256,512]{1,0:T(8,128)(2,1)S(1)} %get-tuple-element.39.refs_3_), channel_id=1, source_target_pairs={{0,24},{4,28},{8,0},{12,4},{16,8},{20,12},{24,16},{28,20},{32,56},... | collective-permute-start | bytes 786440 | tf_op jit(solution)/shard_map/ppermute | solution.py:320
  8.1 1.0 %collective-permute-start.3 = (bf16[256,512]{1,0:T(8,128)(2,1)S(1)}, bf16[256,512]{1,0:T(8,128)(2,1)S(1)}, u32[]{:S(2)}, u32[]{:S(2)}) collective-permute-start(bf16[256,512]{1,0:T(8,128)(2,1)S(1)} %get-tuple-element.39.refs_3_), channel_id=1, source_target_pairs={{0,32},{4,36},{8,40},{12,44},{16,48},{20,52},{24,56},{28,60},{32,0... | collective-permute-start | bytes 786440 | tf_op jit(solution)/shard_map/ppermute | solution.py:320
  9.1 1.5 %collective-permute-start = (bf16[64,2560]{1,0:T(8,128)(2,1)S(1)}, bf16[64,2560]{1,0:T(8,128)(2,1)S(1)}, u32[]{:S(2)}, u32[]{:S(2)}) collective-permute-start(bf16[64,2560]{1,0:T(8,128)(2,1)S(1)} %get-tuple-element.35), channel_id=1, source_target_pairs={{0,1},{1,2},{2,3},{3,0},{4,5},{5,6},{6,7},{7,4},{8,9},{9,10},{10,1... | collective-permute-start | bytes 983048 | tf_op jit(solution)/shard_map/ppermute | solution.py:324
  10.6 1.1 %collective-permute-start.1 = (bf16[64,2560]{1,0:T(8,128)(2,1)S(1)}, bf16[64,2560]{1,0:T(8,128)(2,1)S(1)}, u32[]{:S(2)}, u32[]{:S(2)}) collective-permute-start(bf16[64,2560]{1,0:T(8,128)(2,1)S(1)} %get-tuple-element.36), channel_id=1, source_target_pairs={{0,2},{1,3},{2,0},{3,1},{4,6},{5,7},{6,4},{7,5},{8,10},{9,11},{10,... | collective-permute-start | bytes 983048 | tf_op jit(solution)/shard_map/ppermute | solution.py:324
  12.4 0.6 copy-done.6
  13.0 0.1 fusion.4
  13.1 0.6 copy-done.5
  13.7 0.1 fusion.3
  13.7 0.5 fusion.2
  15.1 0.1 stack.47.refs_0_
  15.2 0.1 stack.52.refs_0_
  15.3 0.1 maximum_multiply_fusion
  15.3 2.2 %collective-permute-start.2 = (bf16[64,2560]{1,0:T(8,128)(2,1)S(1)}, bf16[64,2560]{1,0:T(8,128)(2,1)S(1)}, u32[]{:S(2)}, u32[]{:S(2)}) collective-permute-start(bf16[64,2560]{1,0:T(8,128)(2,1)S(1)} %get-tuple-element.37), channel_id=1, source_target_pairs={{0,3},{1,0},{2,1},{3,2},{4,7},{5,4},{6,5},{7,6},{8,11},{9,8},{10,9... | collective-permute-start | bytes 983048 | tf_op jit(solution)/shard_map/ppermute | solution.py:324
  17.5 0.1 pad_maximum_fusion.2
  17.6 0.0 collective-permute-start.10
  17.6 0.5 collective-permute-start.13
  18.1 1.6 %collective-permute-done.r1 = bf16[64,2560]{1,0:T(8,128)(2,1)S(1)} collective-permute-done((bf16[64,2560]{1,0:T(8,128)(2,1)S(1)}, bf16[64,2560]{1,0:T(8,128)(2,1)S(1)}, u32[]{:S(2)}, u32[]{:S(2)}) %collective-permute-start) | collective-permute-done | bytes 327712 | tf_op jit(solution)/shard_map/ppermute | solution.py:324
  19.7 3.0 %collective-permute-done.1.r2 = bf16[64,2560]{1,0:T(8,128)(2,1)S(1)} collective-permute-done((bf16[64,2560]{1,0:T(8,128)(2,1)S(1)}, bf16[64,2560]{1,0:T(8,128)(2,1)S(1)}, u32[]{:S(2)}, u32[]{:S(2)}) %collective-permute-start.1) | collective-permute-done | bytes 327712 | tf_op jit(solution)/shard_map/ppermute | solution.py:324
  22.8 0.1 fusion
  22.9 4.8 %collective-permute-done.2.r3 = bf16[64,2560]{1,0:T(8,128)(2,1)S(1)} collective-permute-done((bf16[64,2560]{1,0:T(8,128)(2,1)S(1)}, bf16[64,2560]{1,0:T(8,128)(2,1)S(1)}, u32[]{:S(2)}, u32[]{:S(2)}) %collective-permute-start.2) | collective-permute-done | bytes 327712 | tf_op jit(solution)/shard_map/ppermute | solution.py:324
  27.7 1.9 %collective-permute-start.6 = (bf16[256,512]{1,0:T(8,128)(2,1)S(1)}, bf16[256,512]{1,0:T(8,128)(2,1)S(1)}, u32[]{:S(2)}, u32[]{:S(2)}) collective-permute-start(bf16[256,512]{1,0:T(8,128)(2,1)S(1)} %get-tuple-element.39.refs_3_), channel_id=1, source_target_pairs={{0,16},{4,20},{8,24},{12,28},{16,0},{20,4},{24,8},{28,12},{32,48},... | collective-permute-start | bytes 786440 | tf_op jit(solution)/shard_map/ppermute | solution.py:320
  29.6 1.3 %prep.1 = (bf16[2048,128]{1,0:T(8,128)(2,1)S(1)}, bf16[2048,128]{1,0:T(8,128)(2,1)S(1)}, bf16[256,512]{1,0:T(8,128)(2,1)S(1)}) custom-call(s32[1]{0:T(128)} %bitcast.meta, bf16[64,2560]{1,0:T(8,128)(2,1)S(1)} %get-tuple-element.34.own, bf16[64,2560]{1,0:T(8,128)(2,1)S(1)} %collective-permute-done.r1, bf16[64,2560]{1,0:T(8,128)(2,1)S(1)} %collective-permute-done.1.r2, ...), custom_call_target="tpu_custom_call" | custom-call | flops 1000000000 | bytes 3000000 | tf_op jit(solution)/shard_map/prep/pallas_call | solution.py:91
  30.9 1.7 %collective-permute-start.7 = (bf16[256,512]{1,0:T(8,128)(2,1)S(1)}, bf16[256,512]{1,0:T(8,128)(2,1)S(1)}, u32[]{:S(2)}, u32[]{:S(2)}) collective-permute-start(bf16[256,512]{1,0:T(8,128)(2,1)S(1)} %collective-permute-done.3.refs_4_), channel_id=1, source_target_pairs={{0,16},{4,20},{8,24},{12,28},{16,0},{20,4},{24,8},{28,12},{32,48},... | collective-permute-start | bytes 786440 | tf_op jit(solution)/shard_map/ppermute | solution.py:320
  32.6 3.0 %collective-permute-start.5 = (bf16[256,512]{1,0:T(8,128)(2,1)S(1)}, bf16[256,512]{1,0:T(8,128)(2,1)S(1)}, u32[]{:S(2)}, u32[]{:S(2)}) collective-permute-start(bf16[256,512]{1,0:T(8,128)(2,1)S(1)} %collective-permute-done.3.refs_4_), channel_id=1, source_target_pairs={{0,24},{4,28},{8,0},{12,4},{16,8},{20,12},{24,16},{28,20},{32,56},... | collective-permute-start | bytes 786440 | tf_op jit(solution)/shard_map/ppermute | solution.py:320
  35.6 5.2 %attend.4 = (f32[2048,128]{1,0:T(8,128)S(1)}, f32[2048,128]{1,0:T(8,128)S(1)}, f32[2048,128]{1,0:T(8,128)S(1)}) custom-call(s32[8]{0:T(128)S(1)} %stack.52.refs_0_, bf16[2048,128]{1,0:T(8,128)(2,1)S(1)} %get-tuple-element.38.refs_1_, bf16[256,512]{1,0:T(8,128)(2,1)S(1)} %get-tuple-element.40.refs_2_, bf16[256,512]{1,0:T(8,128)(2,1)S(1)} %get-tuple-element.39.refs_3_, ...), custom_call_target="tpu_custom_call" | custom-call | flops 4831838208 | bytes 4194304 | tf_op jit(solution)/shard_map/attend/pallas_call | solution.py:272
  40.8 3.3 %collective-permute-done.7.refs_5_ = bf16[256,512]{1,0:T(8,128)(2,1)S(1)} collective-permute-done((bf16[256,512]{1,0:T(8,128)(2,1)S(1)}, bf16[256,512]{1,0:T(8,128)(2,1)S(1)}, u32[]{:S(2)}, u32[]{:S(2)}) %collective-permute-start.7) | collective-permute-done | bytes 262176 | tf_op jit(solution)/shard_map/ppermute | solution.py:320
  44.1 4.6 %collective-permute-done.5.refs_3_ = bf16[256,512]{1,0:T(8,128)(2,1)S(1)} collective-permute-done((bf16[256,512]{1,0:T(8,128)(2,1)S(1)}, bf16[256,512]{1,0:T(8,128)(2,1)S(1)}, u32[]{:S(2)}, u32[]{:S(2)}) %collective-permute-start.5) | collective-permute-done | bytes 262176 | tf_op jit(solution)/shard_map/ppermute | solution.py:320
  48.6 0.0 collective-permute-start.14
  48.6 0.5 collective-permute-start.15
  49.2 0.5 collective-permute-start.17
  49.6 5.0 %attend.6 = (f32[2048,128]{1,0:T(8,128)S(1)}, f32[2048,128]{1,0:T(8,128)S(1)}, f32[2048,128]{1,0:T(8,128)S(1)}) custom-call(s32[8]{0:T(128)S(1)} %stack.52.refs_0_, bf16[2048,128]{1,0:T(8,128)(2,1)S(1)} %get-tuple-element.55.refs_1_, bf16[256,512]{1,0:T(8,128)(2,1)S(1)} %get-tuple-element.40.refs_2_, bf16[256,512]{1,0:T(8,128)(2,1)S(1)} %get-tuple-element.39.refs_3_, ...), custom_call_target="tpu_custom_call" | custom-call | flops 4831838208 | bytes 4194304 | tf_op jit(solution)/shard_map/attend/pallas_call | solution.py:272
  54.7 8.0 %attend.5 = (bf16[64,1024]{1,0:T(8,128)(2,1)S(1)}, bf16[64,1024]{1,0:T(8,128)(2,1)S(1)}, bf16[64,1024]{1,0:T(8,128)(2,1)S(1)}, bf16[64,1024]{1,0:T(8,128)(2,1)S(1)}) custom-call(s32[8]{0:T(128)S(1)} %stack.47.refs_0_, bf16[2048,128]{1,0:T(8,128)(2,1)S(1)} %get-tuple-element.38.refs_1_, bf16[256,512]{1,0:T(8,128)(2,1)S(1)} %collective-permute-done.4.refs_2_, ...), custom_call_target="tpu_custom_call" | custom-call | flops 4294967296 | bytes 4194304 | tf_op jit(solution)/shard_map/attend/pallas_call | solution.py:272
  62.7 0.1 collective-permute-start.18
  62.8 3.2 %collective-permute-start.19 = (bf16[64,1024]{1,0:T(8,128)(2,1)S(1)}, bf16[64,1024]{1,0:T(8,128)(2,1)S(1)}, u32[]{:S(2)}, u32[]{:S(2)}) collective-permute-start(bf16[64,1024]{1,0:T(8,128)(2,1)S(1)} %get-tuple-element.53), channel_id=1, source_target_pairs={{0,2},{1,3},{2,0},{3,1},{4,6},{5,7},{6,4},{7,5},{8,10},{9,11},{10,... | collective-permute-start | bytes 393224 | tf_op jit(solution)/shard_map/ppermute | solution.py:324
  66.0 7.8 %attend.7 = (bf16[64,1024]{1,0:T(8,128)(2,1)S(1)}, bf16[64,1024]{1,0:T(8,128)(2,1)S(1)}, bf16[64,1024]{1,0:T(8,128)(2,1)S(1)}, bf16[64,1024]{1,0:T(8,128)(2,1)S(1)}) custom-call(s32[8]{0:T(128)S(1)} %stack.47.refs_0_, bf16[2048,128]{1,0:T(8,128)(2,1)S(1)} %get-tuple-element.55.refs_1_, bf16[256,512]{1,0:T(8,128)(2,1)S(1)} %collective-permute-done.4.refs_2_, ...), custom_call_target="tpu_custom_call" | custom-call | flops 4294967296 | bytes 4194304 | tf_op jit(solution)/shard_map/attend/pallas_call | solution.py:272
  73.8 2.1 %collective-permute-start.21 = (bf16[64,1024]{1,0:T(8,128)(2,1)S(1)}, bf16[64,1024]{1,0:T(8,128)(2,1)S(1)}, u32[]{:S(2)}, u32[]{:S(2)}) collective-permute-start(bf16[64,1024]{1,0:T(8,128)(2,1)S(1)} %get-tuple-element.60), channel_id=1, source_target_pairs={{0,1},{1,2},{2,3},{3,0},{4,5},{5,6},{6,7},{7,4},{8,9},{9,10},{10,1... | collective-permute-start | bytes 393224 | tf_op jit(solution)/shard_map/ppermute | solution.py:324
  75.9 1.6 %collective-permute-start.22 = (bf16[64,1024]{1,0:T(8,128)(2,1)S(1)}, bf16[64,1024]{1,0:T(8,128)(2,1)S(1)}, u32[]{:S(2)}, u32[]{:S(2)}) collective-permute-start(bf16[64,1024]{1,0:T(8,128)(2,1)S(1)} %get-tuple-element.61), channel_id=1, source_target_pairs={{0,2},{1,3},{2,0},{3,1},{4,6},{5,7},{6,4},{7,5},{8,10},{9,11},{10,... | collective-permute-start | bytes 393224 | tf_op jit(solution)/shard_map/ppermute | solution.py:324
  77.5 0.7 collective-permute-start.23
  78.2 2.8 %collective-permute-done.21.refs_5_ = bf16[64,1024]{1,0:T(8,128)(2,1)S(1)} collective-permute-done((bf16[64,1024]{1,0:T(8,128)(2,1)S(1)}, bf16[64,1024]{1,0:T(8,128)(2,1)S(1)}, u32[]{:S(2)}, u32[]{:S(2)}) %collective-permute-start.21) | collective-permute-done | bytes 131104 | tf_op jit(solution)/shard_map/ppermute | solution.py:324
  81.0 2.1 %collective-permute-done.22.refs_6_ = bf16[64,1024]{1,0:T(8,128)(2,1)S(1)} collective-permute-done((bf16[64,1024]{1,0:T(8,128)(2,1)S(1)}, bf16[64,1024]{1,0:T(8,128)(2,1)S(1)}, u32[]{:S(2)}, u32[]{:S(2)}) %collective-permute-start.22) | collective-permute-done | bytes 131104 | tf_op jit(solution)/shard_map/ppermute | solution.py:324
  83.1 1.3 %collective-permute-done.23.refs_7_ = bf16[64,1024]{1,0:T(8,128)(2,1)S(1)} collective-permute-done((bf16[64,1024]{1,0:T(8,128)(2,1)S(1)}, bf16[64,1024]{1,0:T(8,128)(2,1)S(1)}, u32[]{:S(2)}, u32[]{:S(2)}) %collective-permute-start.23) | collective-permute-done | bytes 131104 | tf_op jit(solution)/shard_map/ppermute | solution.py:324
  84.4 1.0 %assemble.1 = bf16[64,8192]{1,0:T(8,128)(2,1)} custom-call(s32[1]{0:T(128)} %bitcast.meta, bf16[64,1024]{1,0:T(8,128)(2,1)S(1)} %get-tuple-element.51.refs_0_, bf16[64,1024]{1,0:T(8,128)(2,1)S(1)} %collective-permute-done.18.refs_1_, bf16[64,1024]{1,0:T(8,128)(2,1)S(1)} %collective-permute-done.19.refs_2_, ...), custom_call_target="tpu_custom_call" | custom-call | tf_op jit(solution)/shard_map/assemble/pallas_call | solution.py:299
  (32 shorter events, 0.1 us)
Async XLA Ops:
  0.0 1.2 %copy-start = (bf16[64,8192]{1,0:T(8,128)(2,1)S(1)}, bf16[64,8192]{1,0:T(8,128)(2,1)}, u32[]{:S(2)}) copy-start(bf16[64,8192]{1,0:T(8,128)(2,1)} %queries.1) | copy-start | bytes 3145732
  1.2 0.9 %copy-start.1 = (bf16[256,256]{1,0:T(8,128)(2,1)S(1)}, bf16[256,256]{1,0:T(8,128)(2,1)}, u32[]{:S(2)}) copy-start(bf16[256,256]{1,0:T(8,128)(2,1)} %pk.1) | copy-start | bytes 393220
  2.1 0.9 %copy-start.2 = (bf16[256,256]{1,0:T(8,128)(2,1)S(1)}, bf16[256,256]{1,0:T(8,128)(2,1)}, u32[]{:S(2)}) copy-start(bf16[256,256]{1,0:T(8,128)(2,1)} %pv.1) | copy-start | bytes 393220
  3.0 0.9 %copy-start.3 = (bf16[64,1024]{1,0:T(8,128)(2,1)S(1)}, bf16[64,1024]{1,0:T(8,128)(2,1)}, u32[]{:S(2)}) copy-start(bf16[64,1024]{1,0:T(8,128)(2,1)} %rk.1) | copy-start | bytes 393220
  3.9 0.9 %copy-start.4 = (bf16[64,1024]{1,0:T(8,128)(2,1)S(1)}, bf16[64,1024]{1,0:T(8,128)(2,1)}, u32[]{:S(2)}) copy-start(bf16[64,1024]{1,0:T(8,128)(2,1)} %rv.1) | copy-start | bytes 393220
  5.0 10.3 %collective-permute-start.9 = (bf16[256,512]{1,0:T(8,128)(2,1)S(1)}, bf16[256,512]{1,0:T(8,128)(2,1)S(1)}, u32[]{:S(2)}, u32[]{:S(2)}) collective-permute-start(bf16[256,512]{1,0:T(8,128)(2,1)S(1)} %get-tuple-element.39.refs_3_), channel_id=1, source_target_pairs={{0,24},{4,28},{8,0},{12,4},{16,8},{20,12},{24,16},{28,20},{32,56},... | collective-permute-start | bytes 786440 | tf_op jit(solution)/shard_map/ppermute | solution.py:320
  8.1 9.5 %collective-permute-start.8 = (bf16[256,512]{1,0:T(8,128)(2,1)S(1)}, bf16[256,512]{1,0:T(8,128)(2,1)S(1)}, u32[]{:S(2)}, u32[]{:S(2)}) collective-permute-start(bf16[256,512]{1,0:T(8,128)(2,1)S(1)} %get-tuple-element.39.refs_3_), channel_id=1, source_target_pairs={{0,8},{4,12},{8,16},{12,20},{16,24},{20,28},{24,0},{28,4},{32,40},... | collective-permute-start | bytes 786440 | tf_op jit(solution)/shard_map/ppermute | solution.py:320
  8.1 9.5 %collective-permute-start.3 = (bf16[256,512]{1,0:T(8,128)(2,1)S(1)}, bf16[256,512]{1,0:T(8,128)(2,1)S(1)}, u32[]{:S(2)}, u32[]{:S(2)}) collective-permute-start(bf16[256,512]{1,0:T(8,128)(2,1)S(1)} %get-tuple-element.39.refs_3_), channel_id=1, source_target_pairs={{0,32},{4,36},{8,40},{12,44},{16,48},{20,52},{24,56},{28,60},{32,0... | collective-permute-start | bytes 786440 | tf_op jit(solution)/shard_map/ppermute | solution.py:320
  9.1 10.7 %collective-permute-start = (bf16[64,2560]{1,0:T(8,128)(2,1)S(1)}, bf16[64,2560]{1,0:T(8,128)(2,1)S(1)}, u32[]{:S(2)}, u32[]{:S(2)}) collective-permute-start(bf16[64,2560]{1,0:T(8,128)(2,1)S(1)} %get-tuple-element.35), channel_id=1, source_target_pairs={{0,1},{1,2},{2,3},{3,0},{4,5},{5,6},{6,7},{7,4},{8,9},{9,10},{10,1... | collective-permute-start | bytes 983048 | tf_op jit(solution)/shard_map/ppermute | solution.py:324
  10.6 12.2 %collective-permute-start.1 = (bf16[64,2560]{1,0:T(8,128)(2,1)S(1)}, bf16[64,2560]{1,0:T(8,128)(2,1)S(1)}, u32[]{:S(2)}, u32[]{:S(2)}) collective-permute-start(bf16[64,2560]{1,0:T(8,128)(2,1)S(1)} %get-tuple-element.36), channel_id=1, source_target_pairs={{0,2},{1,3},{2,0},{3,1},{4,6},{5,7},{6,4},{7,5},{8,10},{9,11},{10,... | collective-permute-start | bytes 983048 | tf_op jit(solution)/shard_map/ppermute | solution.py:324
  12.4 0.7 copy-start.6
  13.0 0.7 copy-start.5
  15.3 12.4 %collective-permute-start.2 = (bf16[64,2560]{1,0:T(8,128)(2,1)S(1)}, bf16[64,2560]{1,0:T(8,128)(2,1)S(1)}, u32[]{:S(2)}, u32[]{:S(2)}) collective-permute-start(bf16[64,2560]{1,0:T(8,128)(2,1)S(1)} %get-tuple-element.37), channel_id=1, source_target_pairs={{0,3},{1,0},{2,1},{3,2},{4,7},{5,4},{6,5},{7,6},{8,11},{9,8},{10,9... | collective-permute-start | bytes 983048 | tf_op jit(solution)/shard_map/ppermute | solution.py:324
  17.6 13.3 %collective-permute-start.10 = (bf16[256,512]{1,0:T(8,128)(2,1)S(1)}, bf16[256,512]{1,0:T(8,128)(2,1)S(1)}, u32[]{:S(2)}, u32[]{:S(2)}) collective-permute-start(bf16[256,512]{1,0:T(8,128)(2,1)S(1)} %get-tuple-element.39.refs_3_), channel_id=1, source_target_pairs={{0,4},{4,0},{8,12},{12,8},{16,20},{20,16},{24,28},{28,24},{32,36},... | collective-permute-start | bytes 786440 | tf_op jit(solution)/shard_map/ppermute | solution.py:320
  17.6 15.0 %collective-permute-start.13 = (bf16[256,512]{1,0:T(8,128)(2,1)S(1)}, bf16[256,512]{1,0:T(8,128)(2,1)S(1)}, u32[]{:S(2)}, u32[]{:S(2)}) collective-permute-start(bf16[256,512]{1,0:T(8,128)(2,1)S(1)} %collective-permute-done.9.refs_6_), channel_id=1, source_target_pairs={{0,4},{4,0},{8,12},{12,8},{16,20},{20,16},{24,28},{28,24},{32,36},... | collective-permute-start | bytes 786440 | tf_op jit(solution)/shard_map/ppermute | solution.py:320
  19.7 15.8 %collective-permute-start.12 = (bf16[256,512]{1,0:T(8,128)(2,1)S(1)}, bf16[256,512]{1,0:T(8,128)(2,1)S(1)}, u32[]{:S(2)}, u32[]{:S(2)}) collective-permute-start(bf16[256,512]{1,0:T(8,128)(2,1)S(1)} %collective-permute-done.8.refs_5_), channel_id=1, source_target_pairs={{0,4},{4,0},{8,12},{12,8},{16,20},{20,16},{24,28},{28,24},{32,36},... | collective-permute-start | bytes 786440 | tf_op jit(solution)/shard_map/ppermute | solution.py:320
  22.8 12.8 %collective-permute-start.11 = (bf16[256,512]{1,0:T(8,128)(2,1)S(1)}, bf16[256,512]{1,0:T(8,128)(2,1)S(1)}, u32[]{:S(2)}, u32[]{:S(2)}) collective-permute-start(bf16[256,512]{1,0:T(8,128)(2,1)S(1)} %collective-permute-done.3.refs_4_), channel_id=1, source_target_pairs={{0,4},{4,0},{8,12},{12,8},{16,20},{20,16},{24,28},{28,24},{32,36},... | collective-permute-start | bytes 786440 | tf_op jit(solution)/shard_map/ppermute | solution.py:320
  27.7 13.1 %collective-permute-start.6 = (bf16[256,512]{1,0:T(8,128)(2,1)S(1)}, bf16[256,512]{1,0:T(8,128)(2,1)S(1)}, u32[]{:S(2)}, u32[]{:S(2)}) collective-permute-start(bf16[256,512]{1,0:T(8,128)(2,1)S(1)} %get-tuple-element.39.refs_3_), channel_id=1, source_target_pairs={{0,16},{4,20},{8,24},{12,28},{16,0},{20,4},{24,8},{28,12},{32,48},... | collective-permute-start | bytes 786440 | tf_op jit(solution)/shard_map/ppermute | solution.py:320
  30.9 13.1 %collective-permute-start.7 = (bf16[256,512]{1,0:T(8,128)(2,1)S(1)}, bf16[256,512]{1,0:T(8,128)(2,1)S(1)}, u32[]{:S(2)}, u32[]{:S(2)}) collective-permute-start(bf16[256,512]{1,0:T(8,128)(2,1)S(1)} %collective-permute-done.3.refs_4_), channel_id=1, source_target_pairs={{0,16},{4,20},{8,24},{12,28},{16,0},{20,4},{24,8},{28,12},{32,48},... | collective-permute-start | bytes 786440 | tf_op jit(solution)/shard_map/ppermute | solution.py:320
  32.6 16.0 %collective-permute-start.5 = (bf16[256,512]{1,0:T(8,128)(2,1)S(1)}, bf16[256,512]{1,0:T(8,128)(2,1)S(1)}, u32[]{:S(2)}, u32[]{:S(2)}) collective-permute-start(bf16[256,512]{1,0:T(8,128)(2,1)S(1)} %collective-permute-done.3.refs_4_), channel_id=1, source_target_pairs={{0,24},{4,28},{8,0},{12,4},{16,8},{20,12},{24,16},{28,20},{32,56},... | collective-permute-start | bytes 786440 | tf_op jit(solution)/shard_map/ppermute | solution.py:320
  35.6 13.0 %collective-permute-start.4 = (bf16[256,512]{1,0:T(8,128)(2,1)S(1)}, bf16[256,512]{1,0:T(8,128)(2,1)S(1)}, u32[]{:S(2)}, u32[]{:S(2)}) collective-permute-start(bf16[256,512]{1,0:T(8,128)(2,1)S(1)} %collective-permute-done.3.refs_4_), channel_id=1, source_target_pairs={{0,8},{4,12},{8,16},{12,20},{16,24},{20,28},{24,0},{28,4},{32,40},... | collective-permute-start | bytes 786440 | tf_op jit(solution)/shard_map/ppermute | solution.py:320
  48.6 6.0 %collective-permute-start.14 = (bf16[256,512]{1,0:T(8,128)(2,1)S(1)}, bf16[256,512]{1,0:T(8,128)(2,1)S(1)}, u32[]{:S(2)}, u32[]{:S(2)}) collective-permute-start(bf16[256,512]{1,0:T(8,128)(2,1)S(1)} %collective-permute-done.4.refs_2_), channel_id=1, source_target_pairs={{0,4},{4,0},{8,12},{12,8},{16,20},{20,16},{24,28},{28,24},{32,36},... | collective-permute-start | bytes 786440 | tf_op jit(solution)/shard_map/ppermute | solution.py:320
  48.6 6.0 %collective-permute-start.15 = (bf16[256,512]{1,0:T(8,128)(2,1)S(1)}, bf16[256,512]{1,0:T(8,128)(2,1)S(1)}, u32[]{:S(2)}, u32[]{:S(2)}) collective-permute-start(bf16[256,512]{1,0:T(8,128)(2,1)S(1)} %collective-permute-done.5.refs_3_), channel_id=1, source_target_pairs={{0,4},{4,0},{8,12},{12,8},{16,20},{20,16},{24,28},{28,24},{32,36},... | collective-permute-start | bytes 786440 | tf_op jit(solution)/shard_map/ppermute | solution.py:320
  49.1 5.5 %collective-permute-start.16 = (bf16[256,512]{1,0:T(8,128)(2,1)S(1)}, bf16[256,512]{1,0:T(8,128)(2,1)S(1)}, u32[]{:S(2)}, u32[]{:S(2)}) collective-permute-start(bf16[256,512]{1,0:T(8,128)(2,1)S(1)} %collective-permute-done.6.refs_4_), channel_id=1, source_target_pairs={{0,4},{4,0},{8,12},{12,8},{16,20},{20,16},{24,28},{28,24},{32,36},... | collective-permute-start | bytes 786440 | tf_op jit(solution)/shard_map/ppermute | solution.py:320
  49.2 5.5 %collective-permute-start.17 = (bf16[256,512]{1,0:T(8,128)(2,1)S(1)}, bf16[256,512]{1,0:T(8,128)(2,1)S(1)}, u32[]{:S(2)}, u32[]{:S(2)}) collective-permute-start(bf16[256,512]{1,0:T(8,128)(2,1)S(1)} %collective-permute-done.7.refs_5_), channel_id=1, source_target_pairs={{0,4},{4,0},{8,12},{12,8},{16,20},{20,16},{24,28},{28,24},{32,36},... | collective-permute-start | bytes 786440 | tf_op jit(solution)/shard_map/ppermute | solution.py:320
  62.7 14.8 %collective-permute-start.18 = (bf16[64,1024]{1,0:T(8,128)(2,1)S(1)}, bf16[64,1024]{1,0:T(8,128)(2,1)S(1)}, u32[]{:S(2)}, u32[]{:S(2)}) collective-permute-start(bf16[64,1024]{1,0:T(8,128)(2,1)S(1)} %get-tuple-element.52), channel_id=1, source_target_pairs={{0,1},{1,2},{2,3},{3,0},{4,5},{5,6},{6,7},{7,4},{8,9},{9,10},{10,1... | collective-permute-start | bytes 393224 | tf_op jit(solution)/shard_map/ppermute | solution.py:324
  62.8 15.4 %collective-permute-start.19 = (bf16[64,1024]{1,0:T(8,128)(2,1)S(1)}, bf16[64,1024]{1,0:T(8,128)(2,1)S(1)}, u32[]{:S(2)}, u32[]{:S(2)}) collective-permute-start(bf16[64,1024]{1,0:T(8,128)(2,1)S(1)} %get-tuple-element.53), channel_id=1, source_target_pairs={{0,2},{1,3},{2,0},{3,1},{4,6},{5,7},{6,4},{7,5},{8,10},{9,11},{10,... | collective-permute-start | bytes 393224 | tf_op jit(solution)/shard_map/ppermute | solution.py:324
  66.0 12.2 %collective-permute-start.20 = (bf16[64,1024]{1,0:T(8,128)(2,1)S(1)}, bf16[64,1024]{1,0:T(8,128)(2,1)S(1)}, u32[]{:S(2)}, u32[]{:S(2)}) collective-permute-start(bf16[64,1024]{1,0:T(8,128)(2,1)S(1)} %get-tuple-element.54), channel_id=1, source_target_pairs={{0,3},{1,0},{2,1},{3,2},{4,7},{5,4},{6,5},{7,6},{8,11},{9,8},{10,9... | collective-permute-start | bytes 393224 | tf_op jit(solution)/shard_map/ppermute | solution.py:324
  73.8 7.3 %collective-permute-start.21 = (bf16[64,1024]{1,0:T(8,128)(2,1)S(1)}, bf16[64,1024]{1,0:T(8,128)(2,1)S(1)}, u32[]{:S(2)}, u32[]{:S(2)}) collective-permute-start(bf16[64,1024]{1,0:T(8,128)(2,1)S(1)} %get-tuple-element.60), channel_id=1, source_target_pairs={{0,1},{1,2},{2,3},{3,0},{4,5},{5,6},{6,7},{7,4},{8,9},{9,10},{10,1... | collective-permute-start | bytes 393224 | tf_op jit(solution)/shard_map/ppermute | solution.py:324
  75.9 7.3 %collective-permute-start.22 = (bf16[64,1024]{1,0:T(8,128)(2,1)S(1)}, bf16[64,1024]{1,0:T(8,128)(2,1)S(1)}, u32[]{:S(2)}, u32[]{:S(2)}) collective-permute-start(bf16[64,1024]{1,0:T(8,128)(2,1)S(1)} %get-tuple-element.61), channel_id=1, source_target_pairs={{0,2},{1,3},{2,0},{3,1},{4,6},{5,7},{6,4},{7,5},{8,10},{9,11},{10,... | collective-permute-start | bytes 393224 | tf_op jit(solution)/shard_map/ppermute | solution.py:324
  77.5 6.9 %collective-permute-start.23 = (bf16[64,1024]{1,0:T(8,128)(2,1)S(1)}, bf16[64,1024]{1,0:T(8,128)(2,1)S(1)}, u32[]{:S(2)}, u32[]{:S(2)}) collective-permute-start(bf16[64,1024]{1,0:T(8,128)(2,1)S(1)} %get-tuple-element.62), channel_id=1, source_target_pairs={{0,3},{1,0},{2,1},{3,2},{4,7},{5,4},{6,5},{7,6},{8,11},{9,8},{10,9... | collective-permute-start | bytes 393224 | tf_op jit(solution)/shard_map/ppermute | solution.py:324
where the time goes:
time: 87.2 us; the launch traced here: 85.5 us
  Pallas kernels  28.4 us (33%)
  starting transfers between devices  24.7 us (28%)
  waiting for transfers between devices  23.5 us (27%)
  local copies, waits for them, and re-layouts  6.37 us (7%)
  between operations  1.63 us (2%)
    pallas_call x4, Pallas kernels, attend(): pl.pallas_call(functools.partial(attend_kernel, heads, first, last, layou...  25.9 us
    ppermute x9, waiting for transfers between devices, shift(): return lax.ppermute(x, 'tensor', [(i, (i + d) % 4) for i in range(4)])  15.7 us
    ppermute x9, starting transfers between devices, shift(): return lax.ppermute(x, 'tensor', [(i, (i + d) % 4) for i in range(4)])  12.5 us
    ppermute x15, starting transfers between devices, move(): return lax.ppermute(x, 'resp', pairs)  12.2 us
    ppermute x15, waiting for transfers between devices, move(): return lax.ppermute(x, 'resp', pairs)  7.85 us
    unnamed x14, local copies, waits for them, and re-layouts  6.06 us
  transfers between devices with their start and end apart: 24, of which 8 were waited for; matrix products, arithmetic and copies ran while one was open for 1% of the time, Pallas kernels for 22%

commit v1 on v0

--- a/solution.py
+++ b/solution.py
@@ -24,16 +24,26 @@
     return jnp.dot(a, b, preferred_element_type=jnp.float32)
 
 
-def split_kernel(meta, pk, pv, queries, rk, rv, own, q1, q2, q3, kv):
-    t = meta[0]
-    for d, dst in enumerate((own, q1, q2, q3)):
+def split_kernel(meta, pk, pv, queries, rk, rv, own, q1, q2, q3, kv, sems):
+    t = meta[2]
+    copies = []
+
+    def copy(src, dst):
+        copies.append(pltpu.make_async_copy(src, dst, sems.at[len(copies)]))
+        copies[-1].start()
+
+    for d, dst in ((2, q2), (1, q1), (3, q3), (0, own)):
         u = lax.rem(t + d, 4)
-        dst[:, :2048] = queries[:, pl.ds(pl.multiple_of(u * 2048, 2048), 2048)]
-        dst[:, 2048:2304] = rk[:, pl.ds(pl.multiple_of(u * 256, 256), 256)]
-        dst[:, 2304:] = rv[:, pl.ds(pl.multiple_of(u * 256, 256), 256)]
+        copy(
+            queries.at[:, pl.ds(pl.multiple_of(u * 2048, 2048), 2048)], dst.at[:, pl.ds(0, 2048)]
+        )
+        copy(rk.at[:, pl.ds(pl.multiple_of(u * 256, 256), 256)], dst.at[:, pl.ds(2048, 256)])
+        copy(rv.at[:, pl.ds(pl.multiple_of(u * 256, 256), 256)], dst.at[:, pl.ds(2304, 256)])
     for h in range(2):
-        kv[:, h * 256 : h * 256 + 128] = pk[:, h * 128 : (h + 1) * 128]
-        kv[:, h * 256 + 128 : h * 256 + 256] = pv[:, h * 128 : (h + 1) * 128]
+        copy(pk.at[:, pl.ds(h * 128, 128)], kv.at[:, pl.ds(h * 256, 128)])
+        copy(pv.at[:, pl.ds(h * 128, 128)], kv.at[:, pl.ds(h * 256 + 128, 128)])
+    for c in copies:
+        c.wait()
 
 
 def split(meta, *args):
@@ -42,15 +52,16 @@
     return pl.pallas_call(
         split_kernel,
         out_shape=(piece,) * 4 + (jax.ShapeDtypeStruct((256, 512), jnp.bfloat16),),
-        in_specs=[pl.BlockSpec(memory_space=pltpu.SMEM)] + [vmem] * 5,
+        in_specs=[pl.BlockSpec(memory_space=pltpu.SMEM)] + [pl.BlockSpec(memory_space=pl.ANY)] * 5,
         out_specs=(vmem,) * 5,
-        compiler_params=pltpu.CompilerParams(vmem_limit_bytes=16 * MIB),
+        scratch_shapes=[pltpu.SemaphoreType.DMA((16,))],
+        compiler_params=pltpu.CompilerParams(vmem_limit_bytes=56 * MIB),
         name="split",
     )(meta, *args)
 
 
 def prep_kernel(meta, own, r1, r2, r3, aq, bq, ak, bk, q0, q1, rkv):
-    t = meta[0]
+    t = meta[2]
     wide = jnp.ones((256, 128), jnp.bfloat16)
     at = lax.broadcasted_iota(jnp.int32, (128, 128), 0)
     to = lax.broadcasted_iota(jnp.int32, (128, 128), 1)
@@ -109,7 +120,7 @@
     return start
 
 
-def attend_kernel(heads, first, last, layout, *refs):
+def attend_kernel(heads, first, last, layout, where, *refs):
     it = iter(refs)
     meta = next(it)
     qs = [next(it) for _ in heads]
@@ -118,11 +129,13 @@
     states = [[next(it) for _ in range(3)] for _ in heads] if not first else None
     outs = [[next(it) for _ in range(4)] if last else [next(it) for _ in range(3)] for _ in heads]
     kvs, bias, m_s, mx_s, l_s, acc_s, sa, sb, oa, ob, sems = it
-    plen, rlen, t, core = meta[0], meta[1], meta[2], meta[3]
+    plen, rlen, t, r = meta[0], meta[1], meta[2], meta[3]
+    core, y, z = r & 1, (r >> 1) & 3, r >> 3
     chips = 1 + max(i for i, _, _, _ in layout)
+    bases = [((z ^ dz) * 4 + ((y + dy) & 3)) * 512 for dz, dy in where]
     slots, live = [], 0
     for i in range(chips):
-        is_live = (meta[4 + i] < plen).astype(jnp.int32)
+        is_live = (bases[i] < plen).astype(jnp.int32)
         dead = i - live
         slots.append(jnp.where(is_live == 1, live, chips - 1 - dead))
         live = live + is_live
@@ -140,7 +153,7 @@
             copy.start()
             copies.append(copy)
     for i in range(chips):
-        at = lax.broadcasted_iota(jnp.int32, (8, 512), 1) + meta[4 + i]
+        at = lax.broadcasted_iota(jnp.int32, (8, 512), 1) + bases[i]
         bias[slots[i]] = jnp.where(at < plen, 0.0, NEG)
 
     s_bufs, o_bufs = (sa, sb), (oa, ob)
@@ -243,7 +256,7 @@
         finish(n)
 
 
-def attend(heads, first, last, layout, meta, qs, rkv, pieces, states):
+def attend(heads, first, last, layout, where, meta, qs, rkv, pieces, states):
     vmem = pl.BlockSpec(memory_space=pltpu.VMEM)
     anywhere = pl.BlockSpec(memory_space=pl.ANY)
     chips = 1 + max(i for i, _, _, _ in layout)
@@ -270,24 +283,19 @@
         specs += [vmem] * (3 * len(heads))
     keys = chips * 512 + (256 if first else 0)
     return pl.pallas_call(
-        functools.partial(attend_kernel, heads, first, last, layout),
+        functools.partial(attend_kernel, heads, first, last, layout, where),
         out_shape=tuple(out_shape),
         in_specs=specs,
         out_specs=(vmem,) * len(out_shape),
         scratch_shapes=scratch,
         compiler_params=pltpu.CompilerParams(vmem_limit_bytes=32 * MIB),
-        cost_estimate=pl.CostEstimate(
-            flops=8 * 2048 * keys * 128 * len(heads),
-            bytes_accessed=4 * MIB,
-            transcendentals=2048 * keys * len(heads),
-        ),
         name="attend",
     )(*args)
 
 
 def gather_kernel(meta, *refs):
     pieces, out = refs[:8], refs[8]
-    t = meta[0]
+    t = meta[2]
     for n, piece in enumerate(pieces):
         h, d = n // 4, n % 4
         to = pl.multiple_of(lax.rem(t - d + 4, 4) * 2048 + h * 1024, 1024)
@@ -327,12 +335,13 @@
 def per_device(pk, pv, queries, rk, rv, q_gain, k_gain, prompt_len, resp_len):
     plen, rlen = prompt_len[0], resp_len[0]
     t = lax.axis_index("tensor")
-    r = lax.axis_index("resp")
-    core, y, z = r % 2, (r // 2) % 4, r // 8
-
-    *mine, kv = split(jnp.stack([t]), pk, pv, queries, rk, rv)
+    meta = jnp.stack([plen, rlen, t, lax.axis_index("resp")]).astype(jnp.int32)
+
+    *mine, kv = split(meta, pk, pv, queries, rk, rv)
     q_pieces = [mine[0]] + [shift(mine[d], d) for d in (1, 2, 3)]
-    kz, ka, kb, ks = move(kv, 1, 0), move(kv, 0, 1), move(kv, 0, 3), move(kv, 0, 2)
+    kz, ka = move(kv, 1, 0), move(kv, 0, 1)
+    kv, kz = lax.optimization_barrier((kv, kz))
+    kb, ks = move(kv, 0, 3), move(kv, 0, 2)
     kza, kzb, kzs = move(kz, 0, 1), move(kz, 0, 3), move(kz, 0, 2)
 
     half = HEAD // 2
@@ -351,32 +360,25 @@
         c2 * k_gain,
         s2 * jnp.roll(k_gain, half),
     )
-    q0, q1, rkv = prep(jnp.stack([t]), q_pieces, tables)
-
-    def base(dz, dy):
-        return ((z + dz) % 2 * 4 + (y + dy) % 4) * 512
-
-    def meta(chips):
-        return jnp.stack([plen, rlen, t, core] + [base(dz, dy) for dz, dy in chips]).astype(
-            jnp.int32
-        )
+    q0, q1, rkv = prep(meta, q_pieces, tables)
 
     def both(pieces):
         return list(pieces) + [move(x, 0, 0, 1) for x in pieces]
 
     layout = [(i, o, 0, 256) for o in range(2) for i in range(4)]
-    one = both([kv, kz, ka, kb])
-    meta_one = meta([(0, 0), (1, 0), (0, -1), (0, 1)])
-    meta_two = meta([(1, -1), (1, 1), (0, 2), (1, 2)])
-    st0 = attend((0,), True, False, layout, meta_one, (q0,), rkv, one, None)
+    own_set, q_pieces[3] = lax.optimization_barrier(((kv, kz, ka, kb), q_pieces[3]))
+    one = both(own_set)
+    where_one = ((0, 0), (1, 0), (0, 3), (0, 1))
+    where_two = ((1, 3), (1, 1), (0, 2), (1, 2))
+    st0 = attend((0,), True, False, layout, where_one, meta, (q0,), rkv, one, None)
     (kza, kzb, ks, kzs), st0 = lax.optimization_barrier(((kza, kzb, ks, kzs), st0))
     two = both([kza, kzb, ks, kzs])
-    st1 = attend((1,), True, False, layout, meta_one, (q1,), rkv, one, None)
+    st1 = attend((1,), True, False, layout, where_one, meta, (q1,), rkv, one, None)
     pieces = []
     for h, q, st in ((0, q0, st0), (1, q1, st1)):
-        o = attend((h,), False, True, layout, meta_two, (q,), None, two, [st])
+        o = attend((h,), False, True, layout, where_two, meta, (q,), None, two, [st])
         pieces += [o[0]] + [shift(o[d], d) for d in (1, 2, 3)]
-    return assemble(jnp.stack([t]), pieces)
+    return assemble(meta, pieces)
 
 
 def solution(mesh):

time: 87.2 us -> 92.7 us (1.063)
  the two profiles are of different devices: /device:TPU:162 before, /device:TPU:88 now
where the time goes in v1:
time: 92.7 us; the launch traced here: 92.5 us
  Pallas kernels  38.7 us (42%)
  starting transfers between devices  25.5 us (28%)
  waiting for transfers between devices  24.4 us (26%)
  other arithmetic  1.48 us (2%)
  between operations  1.45 us (2%)
  local copies, waits for them, and re-layouts  0.97 us (1%)
    pallas_call x4, Pallas kernels, attend(): pl.pallas_call(functools.partial(attend_kernel, heads, first, last, layou...  31.9 us
    ppermute x9, waiting for transfers between devices, shift(): return lax.ppermute(x, 'tensor', [(i, (i + d) % 4) for i in range(4)])  16.4 us
    ppermute x9, starting transfers between devices, shift(): return lax.ppermute(x, 'tensor', [(i, (i + d) % 4) for i in range(4)])  14.8 us
    ppermute x15, starting transfers between devices, move(): return lax.ppermute(x, 'resp', pairs)  10.7 us
    ppermute x15, waiting for transfers between devices, move(): return lax.ppermute(x, 'resp', pairs)  8.07 us
    pallas_call x1, Pallas kernels, split(): pl.pallas_call(split_kernel, out_shape=(piece,) * 4 + (jax.ShapeDtypeStru...  3.4 us
  transfers between devices with their start and end apart: 24, of which 9 were waited for; matrix products, arithmetic and copies ran while one was open for 1% of the time, Pallas kernels for 28%

profile of v1, /device:TPU:88, one launch (start us, length us, event | category | flops | bytes accessed | tf_op | source)
XLA Modules:
  0.0 92.5 jit_solution(5788460451205965365)
XLA Ops:
  1.3 0.6 pad_add_fusion.meta.refs_0_
  1.9 3.4 %split.1 = (bf16[64,2560]{1,0:T(8,128)(2,1)}, bf16[64,2560]{1,0:T(8,128)(2,1)}, bf16[64,2560]{1,0:T(8,128)(2,1)}, bf16[64,2560]{1,0:T(8,128)(2,1)}, bf16[256,512]{1,0:T(8,128)(2,1)}) custom-call(s32[4]{0:T(128)} %pad_add_fusion.meta.refs_0_, bf16[256,256]{1,0:T(8,128)(2,1)} %pk.1, bf16[256,256]{1,0:T(8,128)(2,1)} %pv.1, bf16[64,8192]{1,0:T(8,128)(2,1)} %queries.1, ...), custom_call_target="tpu_custom_call" | custom-call | tf_op jit(solution)/shard_map/split/pallas_call | solution.py:52
  5.4 2.0 %collective-permute-start.3 = (bf16[256,512]{1,0:T(8,128)(2,1)}, bf16[256,512]{1,0:T(8,128)(2,1)S(1)}, u32[]{:S(2)}, u32[]{:S(2)}) collective-permute-start(bf16[256,512]{1,0:T(8,128)(2,1)} %get-tuple-element.49.refs_3_), channel_id=1, source_target_pairs={{0,32},{4,36},{8,40},{12,44},{16,48},{20,52},{24,56},{28,60},{32,0... | collective-permute-start | bytes 786440 | tf_op jit(solution)/shard_map/ppermute | solution.py:328
  7.4 0.2 collective-permute-start.8
  7.6 1.5 %collective-permute-start = (bf16[64,2560]{1,0:T(8,128)(2,1)}, bf16[64,2560]{1,0:T(8,128)(2,1)S(1)}, u32[]{:S(2)}, u32[]{:S(2)}) collective-permute-start(bf16[64,2560]{1,0:T(8,128)(2,1)} %get-tuple-element.41), channel_id=1, source_target_pairs={{0,1},{1,2},{2,3},{3,0},{4,5},{5,6},{6,7},{7,4},{8,9},{9,10},{10,1... | collective-permute-start | bytes 983048 | tf_op jit(solution)/shard_map/ppermute | solution.py:332
  9.1 2.7 %collective-permute-start.1 = (bf16[64,2560]{1,0:T(8,128)(2,1)}, bf16[64,2560]{1,0:T(8,128)(2,1)S(1)}, u32[]{:S(2)}, u32[]{:S(2)}) collective-permute-start(bf16[64,2560]{1,0:T(8,128)(2,1)} %get-tuple-element.42), channel_id=1, source_target_pairs={{0,2},{1,3},{2,0},{3,1},{4,6},{5,7},{6,4},{7,5},{8,10},{9,11},{10,... | collective-permute-start | bytes 983048 | tf_op jit(solution)/shard_map/ppermute | solution.py:332
  11.8 1.4 %collective-permute-start.2 = (bf16[64,2560]{1,0:T(8,128)(2,1)}, bf16[64,2560]{1,0:T(8,128)(2,1)S(1)}, u32[]{:S(2)}, u32[]{:S(2)}) collective-permute-start(bf16[64,2560]{1,0:T(8,128)(2,1)} %get-tuple-element.43), channel_id=1, source_target_pairs={{0,3},{1,0},{2,1},{3,2},{4,7},{5,4},{6,5},{7,6},{8,11},{9,8},{10,9... | collective-permute-start | bytes 983048 | tf_op jit(solution)/shard_map/ppermute | solution.py:332
  13.3 0.1 fusion.4
  13.3 0.5 collective-permute-done.3.refs_4_
  13.9 1.3 %collective-permute-start.9 = (bf16[256,512]{1,0:T(8,128)(2,1)}, bf16[256,512]{1,0:T(8,128)(2,1)S(1)}, u32[]{:S(2)}, u32[]{:S(2)}) collective-permute-start(bf16[256,512]{1,0:T(8,128)(2,1)} %get-tuple-element.49.refs_3_), channel_id=1, source_target_pairs={{0,24},{4,28},{8,0},{12,4},{16,8},{20,12},{24,16},{28,20},{32,56},... | collective-permute-start | bytes 786440 | tf_op jit(solution)/shard_map/ppermute | solution.py:328
  15.2 0.1 maximum_multiply_fusion
  15.3 0.1 fusion.3
  15.3 0.0 collective-permute-done.8.refs_5_
  15.3 10.3 %collective-permute-done.2.r3 = bf16[64,2560]{1,0:T(8,128)(2,1)S(1)} collective-permute-done((bf16[64,2560]{1,0:T(8,128)(2,1)}, bf16[64,2560]{1,0:T(8,128)(2,1)S(1)}, u32[]{:S(2)}, u32[]{:S(2)}) %collective-permute-start.2) | collective-permute-done | bytes 327712 | tf_op jit(solution)/shard_map/ppermute | solution.py:332
  25.6 0.0 collective-permute-done.9.refs_6_
  25.6 0.0 collective-permute-start.10
  25.6 0.5 collective-permute-start.11
  26.1 0.0 collective-permute-start.12
  26.1 0.1 pad_maximum_fusion.2
  26.2 0.5 fusion.2
  26.8 1.6 %collective-permute-start.4 = (bf16[256,512]{1,0:T(8,128)(2,1)S(1)}, bf16[256,512]{1,0:T(8,128)(2,1)S(1)}, u32[]{:S(2)}, u32[]{:S(2)}) collective-permute-start(bf16[256,512]{1,0:T(8,128)(2,1)S(1)} %collective-permute-done.3.refs_4_), channel_id=1, source_target_pairs={{0,8},{4,12},{8,16},{12,20},{16,24},{20,28},{24,0},{28,4},{32,40},... | collective-permute-start | bytes 786440 | tf_op jit(solution)/shard_map/ppermute | solution.py:328
  28.3 0.5 collective-permute-start.5
  28.9 2.5 %collective-permute-start.6 = (bf16[256,512]{1,0:T(8,128)(2,1)S(1)}, bf16[256,512]{1,0:T(8,128)(2,1)S(1)}, u32[]{:S(2)}, u32[]{:S(2)}) collective-permute-start(bf16[256,512]{1,0:T(8,128)(2,1)S(1)} %copy-done), channel_id=1, source_target_pairs={{0,16},{4,20},{8,24},{12,28},{16,0},{20,4},{24,8},{28,12},{32,48},... | collective-permute-start | bytes 786440 | tf_op jit(solution)/shard_map/ppermute | solution.py:328
  31.4 1.0 %collective-permute-start.7 = (bf16[256,512]{1,0:T(8,128)(2,1)S(1)}, bf16[256,512]{1,0:T(8,128)(2,1)S(1)}, u32[]{:S(2)}, u32[]{:S(2)}) collective-permute-start(bf16[256,512]{1,0:T(8,128)(2,1)S(1)} %collective-permute-done.3.refs_4_), channel_id=1, source_target_pairs={{0,16},{4,20},{8,24},{12,28},{16,0},{20,4},{24,8},{28,12},{32,48},... | collective-permute-start | bytes 786440 | tf_op jit(solution)/shard_map/ppermute | solution.py:328
  32.4 0.1 fusion
  32.6 0.8 copy-done.2
  33.4 1.8 %prep.1 = (bf16[2048,128]{1,0:T(8,128)(2,1)S(1)}, bf16[2048,128]{1,0:T(8,128)(2,1)S(1)}, bf16[256,512]{1,0:T(8,128)(2,1)S(1)}) custom-call(s32[4]{0:T(128)S(1)} %copy-done.1, bf16[64,2560]{1,0:T(8,128)(2,1)S(1)} %copy-done.2, bf16[64,2560]{1,0:T(8,128)(2,1)S(1)} %collective-permute-done.r1, bf16[64,2560]{1,0:T(8,128)(2,1)S(1)} %collective-permute-done.1.r2, ...), custom_call_target="tpu_custom_call" | custom-call | flops 1000000000 | bytes 3000000 | tf_op jit(solution)/shard_map/prep/pallas_call | solution.py:102
  35.2 8.2 %attend.4 = (f32[2048,128]{1,0:T(8,128)S(1)}, f32[2048,128]{1,0:T(8,128)S(1)}, f32[2048,128]{1,0:T(8,128)S(1)}) custom-call(s32[4]{0:T(128)S(1)} %copy-done.1, bf16[2048,128]{1,0:T(8,128)(2,1)S(1)} %get-tuple-element.44.refs_1_, bf16[256,512]{1,0:T(8,128)(2,1)S(1)} %get-tuple-element.48.refs_2_, bf16[256,512]{1,0:T(8,128)(2,1)S(1)} %copy-done, ...), custom_call_target="tpu_custom_call" | custom-call | tf_op jit(solution)/shard_map/attend/pallas_call | solution.py:285
  43.4 5.9 %collective-permute-done.5.refs_3_ = bf16[256,512]{1,0:T(8,128)(2,1)S(1)} collective-permute-done((bf16[256,512]{1,0:T(8,128)(2,1)S(1)}, bf16[256,512]{1,0:T(8,128)(2,1)S(1)}, u32[]{:S(2)}, u32[]{:S(2)}) %collective-permute-start.5) | collective-permute-done | bytes 262176 | tf_op jit(solution)/shard_map/ppermute | solution.py:328
  49.2 0.5 collective-permute-start.15
  49.8 0.1 collective-permute-start.16
  49.8 0.4 collective-permute-start.17
  50.3 0.5 collective-permute-done.14.refs_6_
  50.8 0.4 collective-permute-done.15.refs_7_
  51.2 0.4 collective-permute-done.16.refs_8_
  51.5 0.4 collective-permute-done.17.refs_9_
  51.9 7.8 %attend.5 = (bf16[64,1024]{1,0:T(8,128)(2,1)S(1)}, bf16[64,1024]{1,0:T(8,128)(2,1)S(1)}, bf16[64,1024]{1,0:T(8,128)(2,1)S(1)}, bf16[64,1024]{1,0:T(8,128)(2,1)S(1)}) custom-call(s32[4]{0:T(128)S(1)} %copy-done.1, bf16[2048,128]{1,0:T(8,128)(2,1)S(1)} %get-tuple-element.44.refs_1_, bf16[256,512]{1,0:T(8,128)(2,1)S(1)} %collective-permute-done.4.refs_2_, ...), custom_call_target="tpu_custom_call" | custom-call | tf_op jit(solution)/shard_map/attend/pallas_call | solution.py:285
  59.7 1.8 %collective-permute-start.18 = (bf16[64,1024]{1,0:T(8,128)(2,1)S(1)}, bf16[64,1024]{1,0:T(8,128)(2,1)S(1)}, u32[]{:S(2)}, u32[]{:S(2)}) collective-permute-start(bf16[64,1024]{1,0:T(8,128)(2,1)S(1)} %get-tuple-element.64), channel_id=1, source_target_pairs={{0,1},{1,2},{2,3},{3,0},{4,5},{5,6},{6,7},{7,4},{8,9},{9,10},{10,1... | collective-permute-start | bytes 393224 | tf_op jit(solution)/shard_map/ppermute | solution.py:332
  61.5 8.2 %attend.6 = (f32[2048,128]{1,0:T(8,128)S(1)}, f32[2048,128]{1,0:T(8,128)S(1)}, f32[2048,128]{1,0:T(8,128)S(1)}) custom-call(s32[4]{0:T(128)S(1)} %copy-done.1, bf16[2048,128]{1,0:T(8,128)(2,1)S(1)} %get-tuple-element.67.refs_1_, bf16[256,512]{1,0:T(8,128)(2,1)S(1)} %get-tuple-element.48.refs_2_, bf16[256,512]{1,0:T(8,128)(2,1)S(1)} %copy-done, ...), custom_call_target="tpu_custom_call" | custom-call | tf_op jit(solution)/shard_map/attend/pallas_call | solution.py:285
  69.7 2.5 %collective-permute-start.19 = (bf16[64,1024]{1,0:T(8,128)(2,1)S(1)}, bf16[64,1024]{1,0:T(8,128)(2,1)S(1)}, u32[]{:S(2)}, u32[]{:S(2)}) collective-permute-start(bf16[64,1024]{1,0:T(8,128)(2,1)S(1)} %get-tuple-element.65), channel_id=1, source_target_pairs={{0,2},{1,3},{2,0},{3,1},{4,6},{5,7},{6,4},{7,5},{8,10},{9,11},{10,... | collective-permute-start | bytes 393224 | tf_op jit(solution)/shard_map/ppermute | solution.py:332
  72.2 1.6 %collective-permute-start.20 = (bf16[64,1024]{1,0:T(8,128)(2,1)S(1)}, bf16[64,1024]{1,0:T(8,128)(2,1)S(1)}, u32[]{:S(2)}, u32[]{:S(2)}) collective-permute-start(bf16[64,1024]{1,0:T(8,128)(2,1)S(1)} %get-tuple-element.66), channel_id=1, source_target_pairs={{0,3},{1,0},{2,1},{3,2},{4,7},{5,4},{6,5},{7,6},{8,11},{9,8},{10,9... | collective-permute-start | bytes 393224 | tf_op jit(solution)/shard_map/ppermute | solution.py:332
  73.7 7.8 %attend.7 = (bf16[64,1024]{1,0:T(8,128)(2,1)S(1)}, bf16[64,1024]{1,0:T(8,128)(2,1)S(1)}, bf16[64,1024]{1,0:T(8,128)(2,1)S(1)}, bf16[64,1024]{1,0:T(8,128)(2,1)S(1)}) custom-call(s32[4]{0:T(128)S(1)} %copy-done.1, bf16[2048,128]{1,0:T(8,128)(2,1)S(1)} %get-tuple-element.67.refs_1_, bf16[256,512]{1,0:T(8,128)(2,1)S(1)} %collective-permute-done.4.refs_2_, ...), custom_call_target="tpu_custom_call" | custom-call | tf_op jit(solution)/shard_map/attend/pallas_call | solution.py:285
  81.5 0.5 collective-permute-start.21
  82.0 1.1 %collective-permute-start.22 = (bf16[64,1024]{1,0:T(8,128)(2,1)S(1)}, bf16[64,1024]{1,0:T(8,128)(2,1)S(1)}, u32[]{:S(2)}, u32[]{:S(2)}) collective-permute-start(bf16[64,1024]{1,0:T(8,128)(2,1)S(1)} %get-tuple-element.73), channel_id=1, source_target_pairs={{0,2},{1,3},{2,0},{3,1},{4,6},{5,7},{6,4},{7,5},{8,10},{9,11},{10,... | collective-permute-start | bytes 393224 | tf_op jit(solution)/shard_map/ppermute | solution.py:332
  83.2 1.6 %collective-permute-start.23 = (bf16[64,1024]{1,0:T(8,128)(2,1)S(1)}, bf16[64,1024]{1,0:T(8,128)(2,1)S(1)}, u32[]{:S(2)}, u32[]{:S(2)}) collective-permute-start(bf16[64,1024]{1,0:T(8,128)(2,1)S(1)} %get-tuple-element.74), channel_id=1, source_target_pairs={{0,3},{1,0},{2,1},{3,2},{4,7},{5,4},{6,5},{7,6},{8,11},{9,8},{10,9... | collective-permute-start | bytes 393224 | tf_op jit(solution)/shard_map/ppermute | solution.py:332
  84.8 5.5 %collective-permute-done.21.refs_5_ = bf16[64,1024]{1,0:T(8,128)(2,1)S(1)} collective-permute-done((bf16[64,1024]{1,0:T(8,128)(2,1)S(1)}, bf16[64,1024]{1,0:T(8,128)(2,1)S(1)}, u32[]{:S(2)}, u32[]{:S(2)}) %collective-permute-start.21) | collective-permute-done | bytes 131104 | tf_op jit(solution)/shard_map/ppermute | solution.py:332
  90.3 0.6 collective-permute-done.23.refs_7_
  90.9 1.6 %assemble.1 = bf16[64,8192]{1,0:T(8,128)(2,1)} custom-call(s32[4]{0:T(128)S(1)} %copy-done.1, bf16[64,1024]{1,0:T(8,128)(2,1)S(1)} %get-tuple-element.63.refs_0_, bf16[64,1024]{1,0:T(8,128)(2,1)S(1)} %collective-permute-done.18.refs_1_, bf16[64,1024]{1,0:T(8,128)(2,1)S(1)} %collective-permute-done.19.refs_2_, ...), custom_call_target="tpu_custom_call" | custom-call | tf_op jit(solution)/shard_map/assemble/pallas_call | solution.py:307
  (27 shorter events, 0.1 us)
Async XLA Ops:
  1.9 11.3 %copy-start.4 = (f32[128]{0:T(128)S(1)}, f32[128]{0:T(128)}, u32[]{:S(2)}) copy-start(f32[128]{0:T(128)} %param.14) | copy-start | bytes 1540
  1.9 13.3 %copy-start.3 = (f32[128]{0:T(128)S(1)}, f32[128]{0:T(128)}, u32[]{:S(2)}) copy-start(f32[128]{0:T(128)} %param.15) | copy-start | bytes 1540
  5.4 23.5 %copy-start = (bf16[256,512]{1,0:T(8,128)(2,1)S(1)}, bf16[256,512]{1,0:T(8,128)(2,1)}, u32[]{:S(2)}) copy-start(bf16[256,512]{1,0:T(8,128)(2,1)} %get-tuple-element.49.refs_3_) | copy-start | bytes 786436
  5.4 8.5 %collective-permute-start.3 = (bf16[256,512]{1,0:T(8,128)(2,1)}, bf16[256,512]{1,0:T(8,128)(2,1)S(1)}, u32[]{:S(2)}, u32[]{:S(2)}) collective-permute-start(bf16[256,512]{1,0:T(8,128)(2,1)} %get-tuple-element.49.refs_3_), channel_id=1, source_target_pairs={{0,32},{4,36},{8,40},{12,44},{16,48},{20,52},{24,56},{28,60},{32,0... | collective-permute-start | bytes 786440 | tf_op jit(solution)/shard_map/ppermute | solution.py:328
  7.4 8.0 %collective-permute-start.8 = (bf16[256,512]{1,0:T(8,128)(2,1)}, bf16[256,512]{1,0:T(8,128)(2,1)S(1)}, u32[]{:S(2)}, u32[]{:S(2)}) collective-permute-start(bf16[256,512]{1,0:T(8,128)(2,1)} %get-tuple-element.49.refs_3_), channel_id=1, source_target_pairs={{0,8},{4,12},{8,16},{12,20},{16,24},{20,28},{24,0},{28,4},{32,40},... | collective-permute-start | bytes 786440 | tf_op jit(solution)/shard_map/ppermute | solution.py:328
  7.6 19.2 %collective-permute-start = (bf16[64,2560]{1,0:T(8,128)(2,1)}, bf16[64,2560]{1,0:T(8,128)(2,1)S(1)}, u32[]{:S(2)}, u32[]{:S(2)}) collective-permute-start(bf16[64,2560]{1,0:T(8,128)(2,1)} %get-tuple-element.41), channel_id=1, source_target_pairs={{0,1},{1,2},{2,3},{3,0},{4,5},{5,6},{6,7},{7,4},{8,9},{9,10},{10,1... | collective-permute-start | bytes 983048 | tf_op jit(solution)/shard_map/ppermute | solution.py:332
  9.1 19.3 %collective-permute-start.1 = (bf16[64,2560]{1,0:T(8,128)(2,1)}, bf16[64,2560]{1,0:T(8,128)(2,1)S(1)}, u32[]{:S(2)}, u32[]{:S(2)}) collective-permute-start(bf16[64,2560]{1,0:T(8,128)(2,1)} %get-tuple-element.42), channel_id=1, source_target_pairs={{0,2},{1,3},{2,0},{3,1},{4,6},{5,7},{6,4},{7,5},{8,10},{9,11},{10,... | collective-permute-start | bytes 983048 | tf_op jit(solution)/shard_map/ppermute | solution.py:332
  11.8 13.8 %collective-permute-start.2 = (bf16[64,2560]{1,0:T(8,128)(2,1)}, bf16[64,2560]{1,0:T(8,128)(2,1)S(1)}, u32[]{:S(2)}, u32[]{:S(2)}) collective-permute-start(bf16[64,2560]{1,0:T(8,128)(2,1)} %get-tuple-element.43), channel_id=1, source_target_pairs={{0,3},{1,0},{2,1},{3,2},{4,7},{5,4},{6,5},{7,6},{8,11},{9,8},{10,9... | collective-permute-start | bytes 983048 | tf_op jit(solution)/shard_map/ppermute | solution.py:332
  13.9 11.7 %collective-permute-start.9 = (bf16[256,512]{1,0:T(8,128)(2,1)}, bf16[256,512]{1,0:T(8,128)(2,1)S(1)}, u32[]{:S(2)}, u32[]{:S(2)}) collective-permute-start(bf16[256,512]{1,0:T(8,128)(2,1)} %get-tuple-element.49.refs_3_), channel_id=1, source_target_pairs={{0,24},{4,28},{8,0},{12,4},{16,8},{20,12},{24,16},{28,20},{32,56},... | collective-permute-start | bytes 786440 | tf_op jit(solution)/shard_map/ppermute | solution.py:328
  25.6 3.3 %collective-permute-start.10 = (bf16[256,512]{1,0:T(8,128)(2,1)}, bf16[256,512]{1,0:T(8,128)(2,1)S(1)}, u32[]{:S(2)}, u32[]{:S(2)}) collective-permute-start(bf16[256,512]{1,0:T(8,128)(2,1)} %get-tuple-element.49.refs_3_), channel_id=1, source_target_pairs={{0,4},{4,0},{8,12},{12,8},{16,20},{20,16},{24,28},{28,24},{32,36},... | collective-permute-start | bytes 786440 | tf_op jit(solution)/shard_map/ppermute | solution.py:328
  25.6 5.8 %collective-permute-start.11 = (bf16[256,512]{1,0:T(8,128)(2,1)S(1)}, bf16[256,512]{1,0:T(8,128)(2,1)S(1)}, u32[]{:S(2)}, u32[]{:S(2)}) collective-permute-start(bf16[256,512]{1,0:T(8,128)(2,1)S(1)} %collective-permute-done.3.refs_4_), channel_id=1, source_target_pairs={{0,4},{4,0},{8,12},{12,8},{16,20},{20,16},{24,28},{28,24},{32,36},... | collective-permute-start | bytes 786440 | tf_op jit(solution)/shard_map/ppermute | solution.py:328
  26.1 6.3 %collective-permute-start.12 = (bf16[256,512]{1,0:T(8,128)(2,1)S(1)}, bf16[256,512]{1,0:T(8,128)(2,1)S(1)}, u32[]{:S(2)}, u32[]{:S(2)}) collective-permute-start(bf16[256,512]{1,0:T(8,128)(2,1)S(1)} %collective-permute-done.8.refs_5_), channel_id=1, source_target_pairs={{0,4},{4,0},{8,12},{12,8},{16,20},{20,16},{24,28},{28,24},{32,36},... | collective-permute-start | bytes 786440 | tf_op jit(solution)/shard_map/ppermute | solution.py:328
  26.8 16.6 %collective-permute-start.4 = (bf16[256,512]{1,0:T(8,128)(2,1)S(1)}, bf16[256,512]{1,0:T(8,128)(2,1)S(1)}, u32[]{:S(2)}, u32[]{:S(2)}) collective-permute-start(bf16[256,512]{1,0:T(8,128)(2,1)S(1)} %collective-permute-done.3.refs_4_), channel_id=1, source_target_pairs={{0,8},{4,12},{8,16},{12,20},{16,24},{20,28},{24,0},{28,4},{32,40},... | collective-permute-start | bytes 786440 | tf_op jit(solution)/shard_map/ppermute | solution.py:328
  28.3 20.9 %collective-permute-start.5 = (bf16[256,512]{1,0:T(8,128)(2,1)S(1)}, bf16[256,512]{1,0:T(8,128)(2,1)S(1)}, u32[]{:S(2)}, u32[]{:S(2)}) collective-permute-start(bf16[256,512]{1,0:T(8,128)(2,1)S(1)} %collective-permute-done.3.refs_4_), channel_id=1, source_target_pairs={{0,24},{4,28},{8,0},{12,4},{16,8},{20,12},{24,16},{28,20},{32,56},... | collective-permute-start | bytes 786440 | tf_op jit(solution)/shard_map/ppermute | solution.py:328
  28.9 20.4 %collective-permute-start.6 = (bf16[256,512]{1,0:T(8,128)(2,1)S(1)}, bf16[256,512]{1,0:T(8,128)(2,1)S(1)}, u32[]{:S(2)}, u32[]{:S(2)}) collective-permute-start(bf16[256,512]{1,0:T(8,128)(2,1)S(1)} %copy-done), channel_id=1, source_target_pairs={{0,16},{4,20},{8,24},{12,28},{16,0},{20,4},{24,8},{28,12},{32,48},... | collective-permute-start | bytes 786440 | tf_op jit(solution)/shard_map/ppermute | solution.py:328
  31.4 17.8 %collective-permute-start.7 = (bf16[256,512]{1,0:T(8,128)(2,1)S(1)}, bf16[256,512]{1,0:T(8,128)(2,1)S(1)}, u32[]{:S(2)}, u32[]{:S(2)}) collective-permute-start(bf16[256,512]{1,0:T(8,128)(2,1)S(1)} %collective-permute-done.3.refs_4_), channel_id=1, source_target_pairs={{0,16},{4,20},{8,24},{12,28},{16,0},{20,4},{24,8},{28,12},{32,48},... | collective-permute-start | bytes 786440 | tf_op jit(solution)/shard_map/ppermute | solution.py:328
  32.4 2.8 %collective-permute-start.13 = (bf16[256,512]{1,0:T(8,128)(2,1)S(1)}, bf16[256,512]{1,0:T(8,128)(2,1)S(1)}, u32[]{:S(2)}, u32[]{:S(2)}) collective-permute-start(bf16[256,512]{1,0:T(8,128)(2,1)S(1)} %collective-permute-done.9.refs_6_), channel_id=1, source_target_pairs={{0,4},{4,0},{8,12},{12,8},{16,20},{20,16},{24,28},{28,24},{32,36},... | collective-permute-start | bytes 786440 | tf_op jit(solution)/shard_map/ppermute | solution.py:328
  32.4 1.0 %copy-start.2 = (bf16[64,2560]{1,0:T(8,128)(2,1)S(1)}, bf16[64,2560]{1,0:T(8,128)(2,1)}, u32[]{:S(2)}) copy-start(bf16[64,2560]{1,0:T(8,128)(2,1)} %get-tuple-element.40.own) | copy-start | bytes 983044
  32.6 0.8 copy-start.1
  49.2 1.5 %collective-permute-start.14 = (bf16[256,512]{1,0:T(8,128)(2,1)S(1)}, bf16[256,512]{1,0:T(8,128)(2,1)S(1)}, u32[]{:S(2)}, u32[]{:S(2)}) collective-permute-start(bf16[256,512]{1,0:T(8,128)(2,1)S(1)} %collective-permute-done.4.refs_2_), channel_id=1, source_target_pairs={{0,4},{4,0},{8,12},{12,8},{16,20},{20,16},{24,28},{28,24},{32,36},... | collective-permute-start | bytes 786440 | tf_op jit(solution)/shard_map/ppermute | solution.py:328
  49.2 1.9 %collective-permute-start.15 = (bf16[256,512]{1,0:T(8,128)(2,1)S(1)}, bf16[256,512]{1,0:T(8,128)(2,1)S(1)}, u32[]{:S(2)}, u32[]{:S(2)}) collective-permute-start(bf16[256,512]{1,0:T(8,128)(2,1)S(1)} %collective-permute-done.5.refs_3_), channel_id=1, source_target_pairs={{0,4},{4,0},{8,12},{12,8},{16,20},{20,16},{24,28},{28,24},{32,36},... | collective-permute-start | bytes 786440 | tf_op jit(solution)/shard_map/ppermute | solution.py:328
  49.8 1.8 %collective-permute-start.16 = (bf16[256,512]{1,0:T(8,128)(2,1)S(1)}, bf16[256,512]{1,0:T(8,128)(2,1)S(1)}, u32[]{:S(2)}, u32[]{:S(2)}) collective-permute-start(bf16[256,512]{1,0:T(8,128)(2,1)S(1)} %collective-permute-done.6.refs_4_), channel_id=1, source_target_pairs={{0,4},{4,0},{8,12},{12,8},{16,20},{20,16},{24,28},{28,24},{32,36},... | collective-permute-start | bytes 786440 | tf_op jit(solution)/shard_map/ppermute | solution.py:328
  49.8 2.1 %collective-permute-start.17 = (bf16[256,512]{1,0:T(8,128)(2,1)S(1)}, bf16[256,512]{1,0:T(8,128)(2,1)S(1)}, u32[]{:S(2)}, u32[]{:S(2)}) collective-permute-start(bf16[256,512]{1,0:T(8,128)(2,1)S(1)} %collective-permute-done.7.refs_5_), channel_id=1, source_target_pairs={{0,4},{4,0},{8,12},{12,8},{16,20},{20,16},{24,28},{28,24},{32,36},... | collective-permute-start | bytes 786440 | tf_op jit(solution)/shard_map/ppermute | solution.py:328
  59.7 23.5 %collective-permute-start.18 = (bf16[64,1024]{1,0:T(8,128)(2,1)S(1)}, bf16[64,1024]{1,0:T(8,128)(2,1)S(1)}, u32[]{:S(2)}, u32[]{:S(2)}) collective-permute-start(bf16[64,1024]{1,0:T(8,128)(2,1)S(1)} %get-tuple-element.64), channel_id=1, source_target_pairs={{0,1},{1,2},{2,3},{3,0},{4,5},{5,6},{6,7},{7,4},{8,9},{9,10},{10,1... | collective-permute-start | bytes 393224 | tf_op jit(solution)/shard_map/ppermute | solution.py:332
  69.7 15.1 %collective-permute-start.19 = (bf16[64,1024]{1,0:T(8,128)(2,1)S(1)}, bf16[64,1024]{1,0:T(8,128)(2,1)S(1)}, u32[]{:S(2)}, u32[]{:S(2)}) collective-permute-start(bf16[64,1024]{1,0:T(8,128)(2,1)S(1)} %get-tuple-element.65), channel_id=1, source_target_pairs={{0,2},{1,3},{2,0},{3,1},{4,6},{5,7},{6,4},{7,5},{8,10},{9,11},{10,... | collective-permute-start | bytes 393224 | tf_op jit(solution)/shard_map/ppermute | solution.py:332
  72.2 12.7 %collective-permute-start.20 = (bf16[64,1024]{1,0:T(8,128)(2,1)S(1)}, bf16[64,1024]{1,0:T(8,128)(2,1)S(1)}, u32[]{:S(2)}, u32[]{:S(2)}) collective-permute-start(bf16[64,1024]{1,0:T(8,128)(2,1)S(1)} %get-tuple-element.66), channel_id=1, source_target_pairs={{0,3},{1,0},{2,1},{3,2},{4,7},{5,4},{6,5},{7,6},{8,11},{9,8},{10,9... | collective-permute-start | bytes 393224 | tf_op jit(solution)/shard_map/ppermute | solution.py:332
  81.5 8.8 %collective-permute-start.21 = (bf16[64,1024]{1,0:T(8,128)(2,1)S(1)}, bf16[64,1024]{1,0:T(8,128)(2,1)S(1)}, u32[]{:S(2)}, u32[]{:S(2)}) collective-permute-start(bf16[64,1024]{1,0:T(8,128)(2,1)S(1)} %get-tuple-element.72), channel_id=1, source_target_pairs={{0,1},{1,2},{2,3},{3,0},{4,5},{5,6},{6,7},{7,4},{8,9},{9,10},{10,1... | collective-permute-start | bytes 393224 | tf_op jit(solution)/shard_map/ppermute | solution.py:332
  82.0 8.2 %collective-permute-start.22 = (bf16[64,1024]{1,0:T(8,128)(2,1)S(1)}, bf16[64,1024]{1,0:T(8,128)(2,1)S(1)}, u32[]{:S(2)}, u32[]{:S(2)}) collective-permute-start(bf16[64,1024]{1,0:T(8,128)(2,1)S(1)} %get-tuple-element.73), channel_id=1, source_target_pairs={{0,2},{1,3},{2,0},{3,1},{4,6},{5,7},{6,4},{7,5},{8,10},{9,11},{10,... | collective-permute-start | bytes 393224 | tf_op jit(solution)/shard_map/ppermute | solution.py:332
  83.2 7.7 %collective-permute-start.23 = (bf16[64,1024]{1,0:T(8,128)(2,1)S(1)}, bf16[64,1024]{1,0:T(8,128)(2,1)S(1)}, u32[]{:S(2)}, u32[]{:S(2)}) collective-permute-start(bf16[64,1024]{1,0:T(8,128)(2,1)S(1)} %get-tuple-element.74), channel_id=1, source_target_pairs={{0,3},{1,0},{2,1},{3,2},{4,7},{5,4},{6,5},{7,6},{8,11},{9,8},{10,9... | collective-permute-start | bytes 393224 | tf_op jit(solution)/shard_map/ppermute | solution.py:332

commit v2 on v0

v2 whole, which is shorter than its diff:
```python
import functools

import jax
import jax.numpy as jnp
from jax import lax
from jax.experimental import pallas as pl
from jax.experimental.pallas import tpu as pltpu
from jax.sharding import PartitionSpec as P

HEAD = 128
LENGTH = 256
ROWS = 1024
CHUNK = 1024
LOG2E = 1.4426950408889634
NEG = -1e30
MIB = 1024 * 1024


def nt(a, b):
    return lax.dot_general(a, b, (((1,), (1,)), ((), ())), preferred_element_type=jnp.float32)


def mm(a, b):
    return jnp.dot(a, b, preferred_element_type=jnp.float32)


def split_kernel(pk, pv, queries, rk, rv, own, q1, q2, q3, kv):
    t = lax.axis_index("tensor")
    for h in range(2):
        kv[:, h * 256 : h * 256 + 128] = pk[:, h * 128 : (h + 1) * 128]
        kv[:, h * 256 + 128 : h * 256 + 256] = pv[:, h * 128 : (h + 1) * 128]
    for d, dst in enumerate((own, q1, q2, q3)):
        u = lax.rem(t + d, 4)
        narrow = pl.ds(pl.multiple_of(u * 256, 256), 256)
        dst[:, :2048] = queries[:, pl.ds(pl.multiple_of(u * 2048, 2048), 2048)]
        dst[:, 2048:2304] = rk[:, narrow]
        dst[:, 2304:] = rv[:, narrow]


def split(*args):
    vmem = pl.BlockSpec(memory_space=pltpu.VMEM)
    piece = jax.ShapeDtypeStruct((64, 2560), jnp.bfloat16)
    cache = jax.ShapeDtypeStruct((256, 512), jnp.bfloat16)
    return pl.pallas_call(
        split_kernel,
        out_shape=(piece,) * 4 + (cache,),
        in_specs=[vmem] * 5,
        out_specs=(vmem,) * 5,
        compiler_params=pltpu.CompilerParams(vmem_limit_bytes=54 * MIB),
        name="split",
    )(*args)


def prep_kernel(own, r1, r2, r3, aq, bq, ak, bk, q0, q1, rkv0, rkv1):
    t = lax.axis_index("tensor")
    wide = jnp.ones((256, 128), jnp.bfloat16)
    at = lax.broadcasted_iota(jnp.int32, (128, 128), 0)
    to = lax.broadcasted_iota(jnp.int32, (128, 128), 1)
    swap = jnp.where((at - to == 64) | (to - at == 64), 1.0, 0.0).astype(jnp.bfloat16)

    def rotated(x, a, b):
        f = x.astype(jnp.float32)
        sq = f * f
        hi = sq.astype(jnp.bfloat16)
        lo = (sq - hi.astype(jnp.float32)).astype(jnp.bfloat16)
        total = mm(jnp.concatenate([hi, lo], axis=1), wide)
        r = lax.rsqrt(total * (1.0 / HEAD) + 1e-06)
        return ((f * a + mm(x, swap) * b) * r).astype(jnp.bfloat16)

    for d, piece in enumerate((own, r1, r2, r3)):
        s = lax.rem(t - d + 4, 4)
        p0 = pl.multiple_of(s * 64, 64)
        rows = pl.ds(p0, 64)
        base = (s // 2) * ROWS + lax.rem(s, 2) * 64
        a8 = jnp.concatenate([aq[rows, :]] * 8, axis=0)
        b8 = jnp.concatenate([bq[rows, :]] * 8, axis=0)
        for h, (q, rkv) in enumerate(((q0, rkv0), (q1, rkv1))):
            x = jnp.concatenate(
                [piece[:, (h * 8 + j) * 128 : (h * 8 + j + 1) * 128] for j in range(8)], axis=0
            )
            y = rotated(x, a8, b8)
            for j in range(8):
                q[pl.ds(pl.multiple_of(base + j * 128, 64), 64), :] = y[j * 64 : (j + 1) * 64]
            k = piece[:, 2048 + h * 128 : 2176 + h * 128]
            rkv[rows, 0:128] = rotated(k, ak[rows, :], bk[rows, :])
            rkv[rows, 128:256] = piece[:, 2304 + h * 128 : 2432 + h * 128]


def prep(pieces, tables):
    vmem = pl.BlockSpec(memory_space=pltpu.VMEM)
    q = jax.ShapeDtypeStruct((2048, 128), jnp.bfloat16)
    rkv = jax.ShapeDtypeStruct((256, 256), jnp.bfloat16)
    return pl.pallas_call(
        prep_kernel,
        out_shape=(q, q, rkv, rkv),
        in_specs=[vmem] * 8,
        out_specs=(vmem,) * 4,
        compiler_params=pltpu.CompilerParams(vmem_limit_bytes=16 * MIB),
        cost_estimate=pl.CostEstimate(flops=10**9, bytes_accessed=3 * 10**6, transcendentals=10**6),
        name="prep",
    )(*pieces, *tables)


def lanes(x, f, start):
    for i in range(x.shape[1] // 128):
        start = f(start, x[:, i * 128 : (i + 1) * 128])
    return start


def attend_kernel(heads, first, last, layout, where, *refs):
    it = iter(refs)
    plen_ref, rlen_ref = next(it), next(it)
    qs = [next(it) for _ in heads]
    rkvs = [next(it) for _ in heads] if first else None
    pieces = [next(it) for _ in range(1 + max(n for n, _, _, _ in layout))]
    states = [[next(it) for _ in range(3)] for _ in heads] if not first else None
    outs = [[next(it) for _ in range(4)] if last else [next(it) for _ in range(3)] for _ in heads]
    kvs, bias, m_s, mx_s, l_s, acc_s, sa, sb, oa, ob, sems = it
    plen, rlen = plen_ref[0], rlen_ref[0]
    t, r = lax.axis_index("tensor"), lax.axis_index("resp")
    core, y, z = r & 1, (r >> 1) & 3, r >> 3
    chips = len(where)
    bases = [((z ^ dz) * 4 + ((y + dy) & 3)) * 512 for dz, dy in where]
    slots, live = [], 0
    for i in range(chips):
        is_live = (bases[i] < plen).astype(jnp.int32)
        dead = i - live
        slots.append(jnp.where(is_live == 1, live, chips - 1 - dead))
        live = live + is_live
    steps = (live * 512 + CHUNK - 1) // CHUNK
    copies = []
    for m, (n, i, other, row) in enumerate(layout):
        c = 1 - core if other else core
        to = pl.multiple_of(slots[i] * 512 + c * 256, 256)
        for k, h in enumerate(heads):
            copy = pltpu.make_async_copy(
                pieces[n].at[pl.ds(row, 256), pl.ds(h * 256, 256)],
                kvs.at[k, pl.ds(to, 256), :],
                sems.at[m * len(heads) + k],
            )
            copy.start()
            copies.append(copy)
    for i in range(chips):
        at = lax.broadcasted_iota(jnp.int32, (8, 512), 1) + bases[i]
        bias[slots[i]] = jnp.where(at < plen, 0.0, NEG)

    s_bufs, o_bufs = (sa, sb), (oa, ob)
    tiles = [(k, p) for k in range(len(heads)) for p in range(2)]

    def rows_of(p):
        return slice(p * ROWS, (p + 1) * ROWS)

    def begin1(n):
        k, p = tiles[n]
        if first:
            s = nt(qs[k][rows_of(p), :], rkvs[k][:, :128])
            key = lax.broadcasted_iota(jnp.int32, (ROWS, 256), 1)
            pos = p * 128 + (lax.broadcasted_iota(jnp.int32, (ROWS, 256), 0) & 127)
            s = jnp.where((key <= pos) & (key < rlen), s, NEG)
            o_bufs[n % 2][...] = s
            m_s[...] = jnp.maximum(s[:, :128], s[:, 128:])
        else:
            m_s[...] = states[k][0][rows_of(p), :]

    def pass1(n, c):
        k, p = tiles[n]
        keys = kvs[k, pl.ds(pl.multiple_of(c * CHUNK, CHUNK), CHUNK), 0:128]
        add = jnp.concatenate([bias[2 * c], bias[2 * c + 1]], axis=1)[0:1, :]
        s = nt(qs[k][rows_of(p), :], keys) + add
        s_bufs[n % 2][c] = s
        m_s[...] = lanes(s, jnp.maximum, m_s[...])

    def weigh(s, m):
        return jnp.concatenate(
            [
                jnp.exp2((s[:, i * 128 : (i + 1) * 128] - m) * LOG2E)
                for i in range(s.shape[1] // 128)
            ],
            axis=1,
        )

    def begin2(n):
        k, p = tiles[n]
        m = jnp.broadcast_to(jnp.max(m_s[...], axis=-1, keepdims=True), (ROWS, 128))
        mx_s[...] = m
        if first:
            w = weigh(o_bufs[n % 2][...], m)
            l_s[...] = w[:, :128] + w[:, 128:]
            acc_s[...] = mm(w.astype(jnp.bfloat16), rkvs[k][:, 128:])
        else:
            old = jnp.exp2((states[k][0][rows_of(p), :] - m) * LOG2E)
            l_s[...] = states[k][1][rows_of(p), :] * old
            acc_s[...] = states[k][2][rows_of(p), :] * old

    def pass2(n, c):
        k, _ = tiles[n]
        values = kvs[k, pl.ds(pl.multiple_of(c * CHUNK, CHUNK), CHUNK), 128:256]
        w = weigh(s_bufs[n % 2][c], mx_s[...])
        l_s[...] = lanes(w, jnp.add, l_s[...])
        acc_s[...] += mm(w.astype(jnp.bfloat16), values)

    def finish(n):
        k, p = tiles[n]
        if not last:
            for ref, x in zip(outs[k], (mx_s, l_s, acc_s)):
                ref[rows_of(p), :] = x[...]
            return
        total = jnp.sum(l_s[...], axis=-1, keepdims=True)
        res = acc_s[...] / total
        pos = p * 128 + (lax.broadcasted_iota(jnp.int32, (ROWS, 128), 0) & 127)
        res = jnp.where(pos < rlen, res, 0.0).astype(jnp.bfloat16)
        for half in range(2):
            d = lax.rem(p * 2 + half - t + 4, 4)
            for e in range(4):

                @pl.when(d == e)
                def _():
                    for j in range(8):
                        r = j * 128 + half * 64
                        outs[k][e][:, j * 128 : (j + 1) * 128] = res[r : r + 64]

    begin1(0)
    for copy in copies:
        copy.wait()

    def loop(f):
        lax.fori_loop(0, steps, lambda c, z: (f(c), z)[1], 0)

    loop(lambda c: pass1(0, c))
    for n in range(len(tiles)):
        begin2(n)
        if n + 1 < len(tiles):
            begin1(n + 1)

            def both(c):
                pass1(n + 1, c)
                pass2(n, c)

            loop(both)
        else:
            loop(lambda c: pass2(n, c))
        finish(n)


def attend(heads, first, last, layout, where, lens, qs, rkvs, pieces, states):
    vmem = pl.BlockSpec(memory_space=pltpu.VMEM)
    anywhere = pl.BlockSpec(memory_space=pl.ANY)
    chips = len(where)
    state = jax.ShapeDtypeStruct((2048, 128), jnp.float32)
    if last:
        out_shape = [jax.ShapeDtypeStruct((64, 1024), jnp.bfloat16)] * (4 * len(heads))
    else:
        out_shape = [state] * (3 * len(heads))
    steps = chips * 512 // CHUNK
    f32 = jnp.float32
    scratch = [
        pltpu.VMEM((len(heads), chips * 512, 256), jnp.bfloat16),
        pltpu.VMEM((chips, 8, 512), f32),
        *[pltpu.VMEM((ROWS, 128), f32)] * 4,
        *[pltpu.VMEM((steps, ROWS, CHUNK), f32)] * 2,
        *[pltpu.VMEM((ROWS if first else 8, 256), f32)] * 2,
        pltpu.SemaphoreType.DMA((len(layout) * len(heads),)),
    ]
    args = [*lens, *qs] + (list(rkvs) if first else []) + list(pieces)
    specs = [pl.BlockSpec(memory_space=pltpu.SMEM)] * 2 + [vmem] * len(qs)
    specs += ([vmem] * len(qs) if first else []) + [anywhere] * len(pieces)
    if not first:
        args += [x for s in states for x in s]
        specs += [vmem] * (3 * len(heads))
    keys = chips * 512 + (256 if first else 0)
    return pl.pallas_call(
        functools.partial(attend_kernel, heads, first, last, layout, where),
        out_shape=tuple(out_shape),
        in_specs=specs,
        out_specs=(vmem,) * len(out_shape),
        scratch_shapes=scratch,
        compiler_params=pltpu.CompilerParams(vmem_limit_bytes=40 * MIB),
        cost_estimate=pl.CostEstimate(
            flops=8 * 2048 * keys * 128 * len(heads),
            bytes_accessed=4 * MIB,
            transcendentals=2048 * keys * len(heads),
        ),
        name="attend",
    )(*args)


def gather_kernel(*refs):
    pieces, out = refs[:8], refs[8]
    t = lax.axis_index("tensor")
    for n, piece in enumerate(pieces):
        h, d = n // 4, n % 4
        to = pl.multiple_of(lax.rem(t - d + 4, 4) * 2048 + h * 1024, 1024)
        out[:, pl.ds(to, 1024)] = piece[...]


def assemble(pieces):
    vmem = pl.BlockSpec(memory_space=pltpu.VMEM)
    return pl.pallas_call(
        gather_kernel,
        out_shape=jax.ShapeDtypeStruct((64, 8192), jnp.bfloat16),
        in_specs=[vmem] * 8,
        out_specs=vmem,
        compiler_params=pltpu.CompilerParams(vmem_limit_bytes=16 * MIB),
        name="assemble",
    )(*pieces)


def place(z, y, c):
    return z * 8 + y * 2 + c


def move(x, dz, dy, dc=0):
    pairs = [
        (place(z, y, c), place(z ^ dz, (y + dy) % 4, c ^ dc))
        for z in range(2)
        for y in range(4)
        for c in range(2)
    ]
    return lax.ppermute(x, "resp", pairs)


def shift(x, d):
    return lax.ppermute(x, "tensor", [(i, (i + d) % 4) for i in range(4)])


def per_device(pk, pv, queries, rk, rv, q_gain, k_gain, prompt_len, resp_len):
    plen = prompt_len[0]
    *mine, kv = split(pk, pv, queries, rk, rv)
    q_pieces = [mine[0]] + [shift(mine[d], d) for d in (1, 2, 3)]
    pair = jnp.concatenate([kv, move(kv, 1, 0)], axis=0)
    near, away, opposite = (move(pair, 0, dy) for dy in (1, 3, 2))

    half = HEAD // 2
    pos = (plen + jnp.arange(LENGTH, dtype=jnp.int32)).astype(jnp.float32)
    freqs = jnp.power(
        jnp.float32(1000000.0), -jnp.arange(half).astype(jnp.float32) * (2.0 / HEAD)
    )
    angles = pos[:, None] * freqs[None, :]
    cosine, sine = jnp.cos(angles), jnp.sin(angles)
    c2 = jnp.concatenate([cosine, cosine], axis=1)
    s2 = jnp.concatenate([-sine, sine], axis=1)
    scale = HEAD ** (-0.5)
    tables = (
        c2 * (q_gain * scale),
        s2 * (jnp.roll(q_gain, half) * scale),
        c2 * k_gain,
        s2 * jnp.roll(k_gain, half),
    )
    q0, q1, rkv0, rkv1 = prep(q_pieces, tables)

    def send(o):
        return [o[0]] + [shift(o[d], d) for d in (1, 2, 3)]

    def both(pieces):
        return list(pieces) + [move(x, 0, 0, 1) for x in pieces]

    lens = (prompt_len, resp_len)
    layout = tuple((o, z, o, z * 256) for o in range(2) for z in range(2))
    st = attend(
        (0, 1),
        True,
        False,
        layout,
        ((0, 0), (1, 0)),
        lens,
        (q0, q1),
        (rkv0, rkv1),
        both([pair]),
        None,
    )
    rest, st = lax.optimization_barrier(((near, away, opposite), st))
    rest = both(rest)
    where = tuple((z, dy) for dy in (3, 1, 2) for z in range(2))
    layout = tuple(
        (o * 3 + n, n * 2 + z, o, z * 256) for o in range(2) for n in range(3) for z in range(2)
    )
    pieces = []
    for h, q in enumerate((q0, q1)):
        states = [st[3 * h : 3 * h + 3]]
        pieces += send(attend((h,), False, True, layout, where, lens, (q,), None, rest, states))
    return assemble(pieces)


def solution(mesh):
    rows = P(("group", "resp", "tensor"), None)
    cache = P(("group", "resp"), "tensor")
    in_specs = (cache, cache, rows, rows, rows, P(), P(), P("group"), P(("group", "resp")))
    return jax.shard_map(
        per_device, mesh=mesh, in_specs=in_specs, out_specs=rows, check_vma=False
    )
```

time: 87.2 us -> 80.4 us (0.922)
  the two profiles are of different devices: /device:TPU:162 before, /device:TPU:1 now
where the time goes in v2:
time: 80.4 us; the launch traced here: 79.3 us
  Pallas kernels  34 us (42%)
  starting transfers between devices  22.8 us (28%)
  waiting for transfers between devices  18.5 us (23%)
  local copies, waits for them, and re-layouts  1.78 us (2%)
  between operations  1.42 us (2%)
  other arithmetic  0.84 us (1%)
    pallas_call x3, Pallas kernels, attend(): pl.pallas_call(functools.partial(attend_kernel, heads, first, last, layou...  29 us
    ppermute x9, starting transfers between devices, shift(): return lax.ppermute(x, 'tensor', [(i, (i + d) % 4) for i in range(4)])  12.1 us
    ppermute x8, waiting for transfers between devices, move(): return lax.ppermute(x, 'resp', pairs)  11.2 us
    ppermute x8, starting transfers between devices, move(): return lax.ppermute(x, 'resp', pairs)  10.7 us
    ppermute x9, waiting for transfers between devices, shift(): return lax.ppermute(x, 'tensor', [(i, (i + d) % 4) for i in range(4)])  7.3 us
    pallas_call x1, Pallas kernels, split(): pl.pallas_call(split_kernel, out_shape=(piece,) * 4 + (cache,), in_specs=...  2.71 us
    unnamed x7, local copies, waits for them, and re-layouts  1.61 us
  transfers between devices with their start and end apart: 17, of which 8 were waited for; matrix products, arithmetic and copies ran while one was open for 2% of the time, Pallas kernels for 25%

profile of v2, /device:TPU:1, one launch (start us, length us, event | category | flops | bytes accessed | tf_op | source)
XLA Modules:
  0.0 79.3 jit_solution(6634057799604534167)
XLA Ops:
  0.0 2.7 %split.1 = (bf16[64,2560]{1,0:T(8,128)(2,1)}, bf16[64,2560]{1,0:T(8,128)(2,1)}, bf16[64,2560]{1,0:T(8,128)(2,1)}, bf16[64,2560]{1,0:T(8,128)(2,1)}, bf16[256,512]{1,0:T(8,128)(2,1)}) custom-call(bf16[256,256]{1,0:T(8,128)(2,1)} %pk.1, bf16[256,256]{1,0:T(8,128)(2,1)} %pv.1, bf16[64,8192]{1,0:T(8,128)(2,1)} %queries.1, bf16[64,1024]{1,0:T(8,128)(2,1)} %rk.1, ...), custom_call_target="tpu_custom_call" | custom-call | tf_op jit(solution)/shard_map/split/pallas_call | solution.py:44
  2.7 2.5 %collective-permute-start.3 = (bf16[256,512]{1,0:T(8,128)(2,1)}, bf16[256,512]{1,0:T(8,128)(2,1)S(1)}, u32[]{:S(2)}, u32[]{:S(2)}) collective-permute-start(bf16[256,512]{1,0:T(8,128)(2,1)} %get-tuple-element.42), channel_id=1, source_target_pairs={{0,32},{4,36},{8,40},{12,44},{16,48},{20,52},{24,56},{28,60},{32,0... | collective-permute-start | bytes 786440 | tf_op jit(solution)/shard_map/ppermute | solution.py:319
  5.2 1.2 %collective-permute-start = (bf16[64,2560]{1,0:T(8,128)(2,1)}, bf16[64,2560]{1,0:T(8,128)(2,1)S(1)}, u32[]{:S(2)}, u32[]{:S(2)}) collective-permute-start(bf16[64,2560]{1,0:T(8,128)(2,1)} %get-tuple-element.38), channel_id=1, source_target_pairs={{0,1},{1,2},{2,3},{3,0},{4,5},{5,6},{6,7},{7,4},{8,9},{9,10},{10,1... | collective-permute-start | bytes 983048 | tf_op jit(solution)/shard_map/ppermute | solution.py:323
  6.4 2.4 %collective-permute-start.1 = (bf16[64,2560]{1,0:T(8,128)(2,1)}, bf16[64,2560]{1,0:T(8,128)(2,1)S(1)}, u32[]{:S(2)}, u32[]{:S(2)}) collective-permute-start(bf16[64,2560]{1,0:T(8,128)(2,1)} %get-tuple-element.39), channel_id=1, source_target_pairs={{0,2},{1,3},{2,0},{3,1},{4,6},{5,7},{6,4},{7,5},{8,10},{9,11},{10,... | collective-permute-start | bytes 983048 | tf_op jit(solution)/shard_map/ppermute | solution.py:323
  8.8 1.2 %collective-permute-start.2 = (bf16[64,2560]{1,0:T(8,128)(2,1)}, bf16[64,2560]{1,0:T(8,128)(2,1)S(1)}, u32[]{:S(2)}, u32[]{:S(2)}) collective-permute-start(bf16[64,2560]{1,0:T(8,128)(2,1)} %get-tuple-element.40), channel_id=1, source_target_pairs={{0,3},{1,0},{2,1},{3,2},{4,7},{5,4},{6,5},{7,6},{8,11},{9,8},{10,9... | collective-permute-start | bytes 983048 | tf_op jit(solution)/shard_map/ppermute | solution.py:323
  10.0 0.1 fusion.4
  10.1 1.0 %constant_dynamic-update-slice_fusion.1 = bf16[512,512]{1,0:T(8,128)(2,1)S(1)} fusion(bf16[256,512]{1,0:T(8,128)(2,1)} %get-tuple-element.42), kind=kLoop, calls=%fused_computation.10 | loop fusion | bytes 524288
  11.7 0.0 copy-start.1
  11.7 0.6 copy-done.1
  12.4 0.1 fusion.3
  13.1 0.5 fusion.2
  13.6 0.0 collective-permute-done.3
  13.7 1.9 %collective-permute-start.7 = (bf16[512,512]{1,0:T(8,128)(2,1)S(1)}, bf16[512,512]{1,0:T(8,128)(2,1)S(1)}, u32[]{:S(2)}, u32[]{:S(2)}) collective-permute-start(bf16[512,512]{1,0:T(8,128)(2,1)S(1)} %constant_dynamic-update-slice_fusion.refs_6_), channel_id=1, source_target_pairs={{0,4},{4,0},{8,12},{12,8},{16,20},{20,16},{24,28},{28,24},{32,36},... | collective-permute-start | bytes 1572872 | tf_op jit(solution)/shard_map/ppermute | solution.py:319
  15.6 0.1 maximum_multiply_fusion
  15.6 0.1 pad_maximum_fusion.2
  15.7 0.1 fusion
  15.8 3.0 %collective-permute-start.6 = (bf16[512,512]{1,0:T(8,128)(2,1)S(1)}, bf16[512,512]{1,0:T(8,128)(2,1)S(1)}, u32[]{:S(2)}, u32[]{:S(2)}) collective-permute-start(bf16[512,512]{1,0:T(8,128)(2,1)S(1)} %constant_dynamic-update-slice_fusion.refs_6_), channel_id=1, source_target_pairs={{0,16},{4,20},{8,24},{12,28},{16,0},{20,4},{24,8},{28,12},{32,48},... | collective-permute-start | bytes 1572872 | tf_op jit(solution)/shard_map/ppermute | solution.py:319
  18.9 0.0 collective-permute-done.r1
  18.9 0.8 collective-permute-start.5
  19.6 3.2 %collective-permute-done.1.r2 = bf16[64,2560]{1,0:T(8,128)(2,1)S(1)} collective-permute-done((bf16[64,2560]{1,0:T(8,128)(2,1)}, bf16[64,2560]{1,0:T(8,128)(2,1)S(1)}, u32[]{:S(2)}, u32[]{:S(2)}) %collective-permute-start.1) | collective-permute-done | bytes 327712 | tf_op jit(solution)/shard_map/ppermute | solution.py:323
  22.9 1.3 %collective-permute-start.4 = (bf16[512,512]{1,0:T(8,128)(2,1)S(1)}, bf16[512,512]{1,0:T(8,128)(2,1)S(1)}, u32[]{:S(2)}, u32[]{:S(2)}) collective-permute-start(bf16[512,512]{1,0:T(8,128)(2,1)S(1)} %constant_dynamic-update-slice_fusion.refs_6_), channel_id=1, source_target_pairs={{0,8},{4,12},{8,16},{12,20},{16,24},{20,28},{24,0},{28,4},{32,40},... | collective-permute-start | bytes 1572872 | tf_op jit(solution)/shard_map/ppermute | solution.py:319
  24.2 0.0 collective-permute-done.2.r3
  24.2 1.2 %prep.1 = (bf16[2048,128]{1,0:T(8,128)(2,1)S(1)}, bf16[2048,128]{1,0:T(8,128)(2,1)S(1)}, bf16[256,256]{1,0:T(8,128)(2,1)S(1)}, bf16[256,256]{1,0:T(8,128)(2,1)S(1)}) custom-call(bf16[64,2560]{1,0:T(8,128)(2,1)S(1)} %copy-done, bf16[64,2560]{1,0:T(8,128)(2,1)S(1)} %collective-permute-done.r1, bf16[64,2560]{1,0:T(8,128)(2,1)S(1)} %collective-permute-done.1.r2, ...), custom_call_target="tpu_custom_call" | custom-call | flops 1000000000 | bytes 3000000 | tf_op jit(solution)/shard_map/prep/pallas_call | solution.py:93
  25.4 0.0 collective-permute-done.7.refs_7_
  25.4 8.5 %attend.3 = (f32[2048,128]{1,0:T(8,128)S(1)}, f32[2048,128]{1,0:T(8,128)S(1)}, f32[2048,128]{1,0:T(8,128)S(1)}, f32[2048,128]{1,0:T(8,128)S(1)}, f32[2048,128]{1,0:T(8,128)S(1)}, /*index=5*/f32[2048,128]{1,0:T(8,128)S(1)}) custom-call(s32[1]{0:T(128)} %copy.11.refs_0_, s32[1]{0:T(128)S(6)} %copy.12.refs_1_, bf16[2048,128]{1,0:T(8,128)(2,1)S(1)} %get-tuple-element.41.refs_2_, ...), custom_call_target="tpu_custom_call" | custom-call | flops 5368709120 | bytes 4194304 | tf_op jit(solution)/shard_map/attend/pallas_call | solution.py:271
  33.9 0.0 collective-permute-done.6.refs_5_
  33.9 8.7 %collective-permute-done.5.refs_4_ = bf16[512,512]{1,0:T(8,128)(2,1)S(1)} collective-permute-done((bf16[512,512]{1,0:T(8,128)(2,1)S(1)}, bf16[512,512]{1,0:T(8,128)(2,1)S(1)}, u32[]{:S(2)}, u32[]{:S(2)}) %collective-permute-start.5) | collective-permute-done | bytes 524320 | tf_op jit(solution)/shard_map/ppermute | solution.py:319
  42.6 0.0 collective-permute-done.4.refs_3_
  42.6 0.8 %collective-permute-start.8 = (bf16[512,512]{1,0:T(8,128)(2,1)S(1)}, bf16[512,512]{1,0:T(8,128)(2,1)S(1)}, u32[]{:S(2)}, u32[]{:S(2)}) collective-permute-start(bf16[512,512]{1,0:T(8,128)(2,1)S(1)} %collective-permute-done.4.refs_3_), channel_id=1, source_target_pairs={{0,4},{4,0},{8,12},{12,8},{16,20},{20,16},{24,28},{28,24},{32,36},... | collective-permute-start | bytes 1572872 | tf_op jit(solution)/shard_map/ppermute | solution.py:319
  43.4 0.0 collective-permute-start.9
  43.4 0.5 collective-permute-start.10
  43.9 1.0 %collective-permute-done.8.refs_6_ = bf16[512,512]{1,0:T(8,128)(2,1)S(1)} collective-permute-done((bf16[512,512]{1,0:T(8,128)(2,1)S(1)}, bf16[512,512]{1,0:T(8,128)(2,1)S(1)}, u32[]{:S(2)}, u32[]{:S(2)}) %collective-permute-start.8) | collective-permute-done | bytes 524320 | tf_op jit(solution)/shard_map/ppermute | solution.py:319
  44.9 0.7 collective-permute-done.9.refs_7_
  45.7 0.7 collective-permute-done.10.refs_8_
  46.4 10.2 %attend.5 = (bf16[64,1024]{1,0:T(8,128)(2,1)S(1)}, bf16[64,1024]{1,0:T(8,128)(2,1)S(1)}, bf16[64,1024]{1,0:T(8,128)(2,1)S(1)}, bf16[64,1024]{1,0:T(8,128)(2,1)S(1)}) custom-call(s32[1]{0:T(128)} %copy.11.refs_0_, s32[1]{0:T(128)S(6)} %copy.12.refs_1_, bf16[2048,128]{1,0:T(8,128)(2,1)S(1)} %get-tuple-element.43.refs_3_.refs_2_, ...), custom_call_target="tpu_custom_call" | custom-call | flops 6442450944 | bytes 4194304 | tf_op jit(solution)/shard_map/attend/pallas_call | solution.py:271
  56.7 0.4 collective-permute-start.14
  57.1 0.6 collective-permute-start.15
  57.7 1.9 %collective-permute-start.16 = (bf16[64,1024]{1,0:T(8,128)(2,1)S(1)}, bf16[64,1024]{1,0:T(8,128)(2,1)S(1)}, u32[]{:S(2)}, u32[]{:S(2)}) collective-permute-start(bf16[64,1024]{1,0:T(8,128)(2,1)S(1)} %get-tuple-element.68), channel_id=1, source_target_pairs={{0,3},{1,0},{2,1},{3,2},{4,7},{5,4},{6,5},{7,6},{8,11},{9,8},{10,9... | collective-permute-start | bytes 393224 | tf_op jit(solution)/shard_map/ppermute | solution.py:323
  59.6 10.2 %attend.4 = (bf16[64,1024]{1,0:T(8,128)(2,1)S(1)}, bf16[64,1024]{1,0:T(8,128)(2,1)S(1)}, bf16[64,1024]{1,0:T(8,128)(2,1)S(1)}, bf16[64,1024]{1,0:T(8,128)(2,1)S(1)}) custom-call(s32[1]{0:T(128)} %copy.11.refs_0_, s32[1]{0:T(128)S(6)} %copy.12.refs_1_, bf16[2048,128]{1,0:T(8,128)(2,1)S(1)} %get-tuple-element.41.refs_2_, ...), custom_call_target="tpu_custom_call" | custom-call | flops 6442450944 | bytes 4194304 | tf_op jit(solution)/shard_map/attend/pallas_call | solution.py:271
  69.8 0.5 collective-permute-start.11
  70.3 1.9 %collective-permute-start.12 = (bf16[64,1024]{1,0:T(8,128)(2,1)S(1)}, bf16[64,1024]{1,0:T(8,128)(2,1)S(1)}, u32[]{:S(2)}, u32[]{:S(2)}) collective-permute-start(bf16[64,1024]{1,0:T(8,128)(2,1)S(1)} %get-tuple-element.60), channel_id=1, source_target_pairs={{0,2},{1,3},{2,0},{3,1},{4,6},{5,7},{6,4},{7,5},{8,10},{9,11},{10,... | collective-permute-start | bytes 393224 | tf_op jit(solution)/shard_map/ppermute | solution.py:323
  72.2 2.0 %collective-permute-start.13 = (bf16[64,1024]{1,0:T(8,128)(2,1)S(1)}, bf16[64,1024]{1,0:T(8,128)(2,1)S(1)}, u32[]{:S(2)}, u32[]{:S(2)}) collective-permute-start(bf16[64,1024]{1,0:T(8,128)(2,1)S(1)} %get-tuple-element.61), channel_id=1, source_target_pairs={{0,3},{1,0},{2,1},{3,2},{4,7},{5,4},{6,5},{7,6},{8,11},{9,8},{10,9... | collective-permute-start | bytes 393224 | tf_op jit(solution)/shard_map/ppermute | solution.py:323
  74.2 0.0 collective-permute-done.15.refs_6_
  74.2 0.0 collective-permute-done.16.refs_7_
  74.2 1.8 %collective-permute-done.11.refs_1_ = bf16[64,1024]{1,0:T(8,128)(2,1)S(1)} collective-permute-done((bf16[64,1024]{1,0:T(8,128)(2,1)S(1)}, bf16[64,1024]{1,0:T(8,128)(2,1)S(1)}, u32[]{:S(2)}, u32[]{:S(2)}) %collective-permute-start.11) | collective-permute-done | bytes 131104 | tf_op jit(solution)/shard_map/ppermute | solution.py:323
  76.0 1.2 %collective-permute-done.12.refs_2_ = bf16[64,1024]{1,0:T(8,128)(2,1)S(1)} collective-permute-done((bf16[64,1024]{1,0:T(8,128)(2,1)S(1)}, bf16[64,1024]{1,0:T(8,128)(2,1)S(1)}, u32[]{:S(2)}, u32[]{:S(2)}) %collective-permute-start.12) | collective-permute-done | bytes 131104 | tf_op jit(solution)/shard_map/ppermute | solution.py:323
  77.3 1.0 %collective-permute-done.13.refs_3_ = bf16[64,1024]{1,0:T(8,128)(2,1)S(1)} collective-permute-done((bf16[64,1024]{1,0:T(8,128)(2,1)S(1)}, bf16[64,1024]{1,0:T(8,128)(2,1)S(1)}, u32[]{:S(2)}, u32[]{:S(2)}) %collective-permute-start.13) | collective-permute-done | bytes 131104 | tf_op jit(solution)/shard_map/ppermute | solution.py:323
  78.3 1.0 %assemble.1 = bf16[64,8192]{1,0:T(8,128)(2,1)} custom-call(bf16[64,1024]{1,0:T(8,128)(2,1)S(1)} %get-tuple-element.58.refs_0_, bf16[64,1024]{1,0:T(8,128)(2,1)S(1)} %collective-permute-done.11.refs_1_, bf16[64,1024]{1,0:T(8,128)(2,1)S(1)} %collective-permute-done.12.refs_2_, bf16[64,1024]{1,0:T(8,128)(2,1)S(1)} %collective-permute-done.13.refs_3_, ...), custom_call_target="tpu_custom_call" | custom-call | tf_op jit(solution)/shard_map/assemble/pallas_call | solution.py:298
  (9 shorter events, 0.0 us)
Async XLA Ops:
  2.7 10.9 %collective-permute-start.3 = (bf16[256,512]{1,0:T(8,128)(2,1)}, bf16[256,512]{1,0:T(8,128)(2,1)S(1)}, u32[]{:S(2)}, u32[]{:S(2)}) collective-permute-start(bf16[256,512]{1,0:T(8,128)(2,1)} %get-tuple-element.42), channel_id=1, source_target_pairs={{0,32},{4,36},{8,40},{12,44},{16,48},{20,52},{24,56},{28,60},{32,0... | collective-permute-start | bytes 786440 | tf_op jit(solution)/shard_map/ppermute | solution.py:319
  5.2 13.7 %collective-permute-start = (bf16[64,2560]{1,0:T(8,128)(2,1)}, bf16[64,2560]{1,0:T(8,128)(2,1)S(1)}, u32[]{:S(2)}, u32[]{:S(2)}) collective-permute-start(bf16[64,2560]{1,0:T(8,128)(2,1)} %get-tuple-element.38), channel_id=1, source_target_pairs={{0,1},{1,2},{2,3},{3,0},{4,5},{5,6},{6,7},{7,4},{8,9},{9,10},{10,1... | collective-permute-start | bytes 983048 | tf_op jit(solution)/shard_map/ppermute | solution.py:323
  6.4 3.6 %copy-start.2 = (f32[128]{0:T(128)S(1)}, f32[128]{0:T(128)}, u32[]{:S(2)}) copy-start(f32[128]{0:T(128)} %param.14) | copy-start | bytes 1540
  6.4 16.5 %collective-permute-start.1 = (bf16[64,2560]{1,0:T(8,128)(2,1)}, bf16[64,2560]{1,0:T(8,128)(2,1)S(1)}, u32[]{:S(2)}, u32[]{:S(2)}) collective-permute-start(bf16[64,2560]{1,0:T(8,128)(2,1)} %get-tuple-element.39), channel_id=1, source_target_pairs={{0,2},{1,3},{2,0},{3,1},{4,6},{5,7},{6,4},{7,5},{8,10},{9,11},{10,... | collective-permute-start | bytes 983048 | tf_op jit(solution)/shard_map/ppermute | solution.py:323
  8.8 15.3 %collective-permute-start.2 = (bf16[64,2560]{1,0:T(8,128)(2,1)}, bf16[64,2560]{1,0:T(8,128)(2,1)S(1)}, u32[]{:S(2)}, u32[]{:S(2)}) collective-permute-start(bf16[64,2560]{1,0:T(8,128)(2,1)} %get-tuple-element.40), channel_id=1, source_target_pairs={{0,3},{1,0},{2,1},{3,2},{4,7},{5,4},{6,5},{7,6},{8,11},{9,8},{10,9... | collective-permute-start | bytes 983048 | tf_op jit(solution)/shard_map/ppermute | solution.py:323
  11.7 0.7 copy-start.1
  13.7 11.7 %collective-permute-start.7 = (bf16[512,512]{1,0:T(8,128)(2,1)S(1)}, bf16[512,512]{1,0:T(8,128)(2,1)S(1)}, u32[]{:S(2)}, u32[]{:S(2)}) collective-permute-start(bf16[512,512]{1,0:T(8,128)(2,1)S(1)} %constant_dynamic-update-slice_fusion.refs_6_), channel_id=1, source_target_pairs={{0,4},{4,0},{8,12},{12,8},{16,20},{20,16},{24,28},{28,24},{32,36},... | collective-permute-start | bytes 1572872 | tf_op jit(solution)/shard_map/ppermute | solution.py:319
  15.7 8.5 %copy-start = (bf16[64,2560]{1,0:T(8,128)(2,1)S(1)}, bf16[64,2560]{1,0:T(8,128)(2,1)}, u32[]{:S(2)}) copy-start(bf16[64,2560]{1,0:T(8,128)(2,1)} %get-tuple-element.37.own) | copy-start | bytes 983044
  15.8 18.1 %collective-permute-start.6 = (bf16[512,512]{1,0:T(8,128)(2,1)S(1)}, bf16[512,512]{1,0:T(8,128)(2,1)S(1)}, u32[]{:S(2)}, u32[]{:S(2)}) collective-permute-start(bf16[512,512]{1,0:T(8,128)(2,1)S(1)} %constant_dynamic-update-slice_fusion.refs_6_), channel_id=1, source_target_pairs={{0,16},{4,20},{8,24},{12,28},{16,0},{20,4},{24,8},{28,12},{32,48},... | collective-permute-start | bytes 1572872 | tf_op jit(solution)/shard_map/ppermute | solution.py:319
  18.9 23.8 %collective-permute-start.5 = (bf16[512,512]{1,0:T(8,128)(2,1)S(1)}, bf16[512,512]{1,0:T(8,128)(2,1)S(1)}, u32[]{:S(2)}, u32[]{:S(2)}) collective-permute-start(bf16[512,512]{1,0:T(8,128)(2,1)S(1)} %constant_dynamic-update-slice_fusion.refs_6_), channel_id=1, source_target_pairs={{0,24},{4,28},{8,0},{12,4},{16,8},{20,12},{24,16},{28,20},{32,56},... | collective-permute-start | bytes 1572872 | tf_op jit(solution)/shard_map/ppermute | solution.py:319
  22.9 19.7 %collective-permute-start.4 = (bf16[512,512]{1,0:T(8,128)(2,1)S(1)}, bf16[512,512]{1,0:T(8,128)(2,1)S(1)}, u32[]{:S(2)}, u32[]{:S(2)}) collective-permute-start(bf16[512,512]{1,0:T(8,128)(2,1)S(1)} %constant_dynamic-update-slice_fusion.refs_6_), channel_id=1, source_target_pairs={{0,8},{4,12},{8,16},{12,20},{16,24},{20,28},{24,0},{28,4},{32,40},... | collective-permute-start | bytes 1572872 | tf_op jit(solution)/shard_map/ppermute | solution.py:319
  42.6 2.3 %collective-permute-start.8 = (bf16[512,512]{1,0:T(8,128)(2,1)S(1)}, bf16[512,512]{1,0:T(8,128)(2,1)S(1)}, u32[]{:S(2)}, u32[]{:S(2)}) collective-permute-start(bf16[512,512]{1,0:T(8,128)(2,1)S(1)} %collective-permute-done.4.refs_3_), channel_id=1, source_target_pairs={{0,4},{4,0},{8,12},{12,8},{16,20},{20,16},{24,28},{28,24},{32,36},... | collective-permute-start | bytes 1572872 | tf_op jit(solution)/shard_map/ppermute | solution.py:319
  43.4 2.3 %collective-permute-start.9 = (bf16[512,512]{1,0:T(8,128)(2,1)S(1)}, bf16[512,512]{1,0:T(8,128)(2,1)S(1)}, u32[]{:S(2)}, u32[]{:S(2)}) collective-permute-start(bf16[512,512]{1,0:T(8,128)(2,1)S(1)} %collective-permute-done.5.refs_4_), channel_id=1, source_target_pairs={{0,4},{4,0},{8,12},{12,8},{16,20},{20,16},{24,28},{28,24},{32,36},... | collective-permute-start | bytes 1572872 | tf_op jit(solution)/shard_map/ppermute | solution.py:319
  43.4 3.0 %collective-permute-start.10 = (bf16[512,512]{1,0:T(8,128)(2,1)S(1)}, bf16[512,512]{1,0:T(8,128)(2,1)S(1)}, u32[]{:S(2)}, u32[]{:S(2)}) collective-permute-start(bf16[512,512]{1,0:T(8,128)(2,1)S(1)} %collective-permute-done.6.refs_5_), channel_id=1, source_target_pairs={{0,4},{4,0},{8,12},{12,8},{16,20},{20,16},{24,28},{28,24},{32,36},... | collective-permute-start | bytes 1572872 | tf_op jit(solution)/shard_map/ppermute | solution.py:319
  56.7 15.5 %collective-permute-start.14 = (bf16[64,1024]{1,0:T(8,128)(2,1)S(1)}, bf16[64,1024]{1,0:T(8,128)(2,1)S(1)}, u32[]{:S(2)}, u32[]{:S(2)}) collective-permute-start(bf16[64,1024]{1,0:T(8,128)(2,1)S(1)} %get-tuple-element.66), channel_id=1, source_target_pairs={{0,1},{1,2},{2,3},{3,0},{4,5},{5,6},{6,7},{7,4},{8,9},{9,10},{10,1... | collective-permute-start | bytes 393224 | tf_op jit(solution)/shard_map/ppermute | solution.py:323
  57.1 17.1 %collective-permute-start.15 = (bf16[64,1024]{1,0:T(8,128)(2,1)S(1)}, bf16[64,1024]{1,0:T(8,128)(2,1)S(1)}, u32[]{:S(2)}, u32[]{:S(2)}) collective-permute-start(bf16[64,1024]{1,0:T(8,128)(2,1)S(1)} %get-tuple-element.67), channel_id=1, source_target_pairs={{0,2},{1,3},{2,0},{3,1},{4,6},{5,7},{6,4},{7,5},{8,10},{9,11},{10,... | collective-permute-start | bytes 393224 | tf_op jit(solution)/shard_map/ppermute | solution.py:323
  57.7 16.5 %collective-permute-start.16 = (bf16[64,1024]{1,0:T(8,128)(2,1)S(1)}, bf16[64,1024]{1,0:T(8,128)(2,1)S(1)}, u32[]{:S(2)}, u32[]{:S(2)}) collective-permute-start(bf16[64,1024]{1,0:T(8,128)(2,1)S(1)} %get-tuple-element.68), channel_id=1, source_target_pairs={{0,3},{1,0},{2,1},{3,2},{4,7},{5,4},{6,5},{7,6},{8,11},{9,8},{10,9... | collective-permute-start | bytes 393224 | tf_op jit(solution)/shard_map/ppermute | solution.py:323
  69.8 6.2 %collective-permute-start.11 = (bf16[64,1024]{1,0:T(8,128)(2,1)S(1)}, bf16[64,1024]{1,0:T(8,128)(2,1)S(1)}, u32[]{:S(2)}, u32[]{:S(2)}) collective-permute-start(bf16[64,1024]{1,0:T(8,128)(2,1)S(1)} %get-tuple-element.59), channel_id=1, source_target_pairs={{0,1},{1,2},{2,3},{3,0},{4,5},{5,6},{6,7},{7,4},{8,9},{9,10},{10,1... | collective-permute-start | bytes 393224 | tf_op jit(solution)/shard_map/ppermute | solution.py:323
  70.3 6.9 %collective-permute-start.12 = (bf16[64,1024]{1,0:T(8,128)(2,1)S(1)}, bf16[64,1024]{1,0:T(8,128)(2,1)S(1)}, u32[]{:S(2)}, u32[]{:S(2)}) collective-permute-start(bf16[64,1024]{1,0:T(8,128)(2,1)S(1)} %get-tuple-element.60), channel_id=1, source_target_pairs={{0,2},{1,3},{2,0},{3,1},{4,6},{5,7},{6,4},{7,5},{8,10},{9,11},{10,... | collective-permute-start | bytes 393224 | tf_op jit(solution)/shard_map/ppermute | solution.py:323
  72.2 6.0 %collective-permute-start.13 = (bf16[64,1024]{1,0:T(8,128)(2,1)S(1)}, bf16[64,1024]{1,0:T(8,128)(2,1)S(1)}, u32[]{:S(2)}, u32[]{:S(2)}) collective-permute-start(bf16[64,1024]{1,0:T(8,128)(2,1)S(1)} %get-tuple-element.61), channel_id=1, source_target_pairs={{0,3},{1,0},{2,1},{3,2},{4,7},{5,4},{6,5},{7,6},{8,11},{9,8},{10,9... | collective-permute-start | bytes 393224 | tf_op jit(solution)/shard_map/ppermute | solution.py:323
